TPU v7x, 32 devices: a whole 2x2x4 slice. The times are simulated.
32 devices in a mesh: groups: 2 (over x), blk: 16 (over z, y, core).
Axes of the slice: x: 2, y: 2, z: 4, core: 2. Of those that a mesh axis runs over, the one named last changes fastest.
Arguments:
- queries: bfloat16 [4096, 512], P(('groups', 'blk')), parts along dimension 0, may hold values from -8 to 8
- key_states: bfloat16 [4096, 128], P(('groups', 'blk')), parts along dimension 0, may hold values from -6 to 6
- value_states: bfloat16 [4096, 128], P(('groups', 'blk')), parts along dimension 0, may hold values from -6 to 6
- grad_out: bfloat16 [4096, 512], P(('groups', 'blk')), parts along dimension 0, may hold values from -6 to 6
- tile_mask: int32 [32, 16], P('groups'), parts along dimension 0, may hold values 0 or 1
- block_order: int32 [32], P('groups'), parts along dimension 0, may hold values from 0 to 15, each once
Outputs:
- attended: bfloat16 [4096, 512], P(('groups', 'blk')), parts along dimension 0
- grad_queries: bfloat16 [4096, 512], P(('groups', 'blk')), parts along dimension 0
- grad_keys: float32 [4096, 128], P(('groups', 'blk')), parts along dimension 0
- grad_values: float32 [4096, 128], P(('groups', 'blk')), parts along dimension 0
There are 2 independent parts, one for each index of `groups`. A program takes and returns all parts, laid end to end along the dimension named above; each array names one. Nothing has to cross between parts.
Inputs may be any that keep to these rules, and one draw needn't show every extreme that they name: `block_order`: each block number appears once.
All inputs are finite; a program needn't handle non-finite values.
Results may differ from a plain program's by a relative error of at most 0.04.
Values may be sent and summed in bfloat16 or wider, within the bound.
A program may use at most 64 MiB of HBM per device.

v0:
```python
import jax
import jax.numpy as jnp
from jax import lax
from jax.sharding import PartitionSpec as P

TILE = 128


def passed_along(value, axis, steps):
    count = lax.axis_size(axis)
    pairs = [(source, (source + steps) % count) for source in range(count)]
    return lax.ppermute(value, axis, pairs)


def shards(queries, key_states, value_states, grad_out, tile_mask, block_order):
    cycle_size = lax.axis_size("blk")
    my_index = lax.axis_index("blk")
    tok_rows = key_states.shape[0]
    head_width = key_states.shape[1]
    head_count = queries.shape[1] // head_width
    scaling = head_width ** (-0.5)
    tiles_per = tok_rows // TILE
    tile_total = tile_mask.shape[1]
    offsets = jnp.arange(tok_rows, dtype=jnp.int32)
    my_block = block_order[my_index]
    total_rows = head_count * tok_rows

    def to_rows(features):
        return (
            features.reshape(tok_rows, head_count, head_width)
            .transpose(1, 0, 2)
            .reshape(total_rows, head_width)
        )

    def from_rows(row_form):
        return (
            row_form.reshape(head_count, tok_rows, head_width)
            .transpose(1, 0, 2)
            .reshape(tok_rows, head_count * head_width)
        )

    query_rows = to_rows(queries)
    cot_rows = to_rows(grad_out)

    def mask_for(query_block, key_pos):
        query_pos = query_block * tok_rows + offsets
        tile_rows = lax.dynamic_slice_in_dim(
            tile_mask, query_block * tiles_per, tiles_per, 0
        ).astype(jnp.float32)
        tile_rows = jnp.repeat(tile_rows, TILE, axis=0)
        one_hot = (
            (key_pos // TILE)[:, None] == jnp.arange(tile_total, dtype=jnp.int32)[None, :]
        ).astype(jnp.float32)
        tile_bits = jnp.dot(tile_rows, one_hot.T, preferred_element_type=jnp.float32) > 0.5
        same_tile = (query_pos // TILE)[:, None] == (key_pos // TILE)[None, :]
        allowed = (query_pos[:, None] >= key_pos[None, :]) & (tile_bits | same_tile)
        return jnp.tile(allowed, (head_count, 1))

    def softmax_update(carry_state, key_sub, value_sub, allowed):
        run_max, run_sum, run_acc = carry_state
        scores = (
            jnp.einsum("rd,kd->rk", query_rows, key_sub, preferred_element_type=jnp.float32)
            * scaling
        )
        scores = jnp.where(allowed, scores, -1e30)
        new_max = jnp.maximum(run_max, jnp.max(scores, axis=1))
        weights = jnp.where(allowed, jnp.exp(scores - new_max[:, None]), 0.0)
        factor = jnp.exp(run_max - new_max)
        run_sum = run_sum * factor + jnp.sum(weights, axis=1)
        run_acc = run_acc * factor[:, None] + jnp.dot(
            weights.astype(jnp.bfloat16), value_sub, preferred_element_type=jnp.float32
        )
        return (new_max, run_sum, run_acc)

    def guarded_update(carry_state, key_sub, value_sub, allowed):
        return softmax_update(carry_state, key_sub, value_sub, allowed)

    start_state = (
        jnp.full((total_rows,), -1e30, jnp.float32),
        jnp.zeros((total_rows,), jnp.float32),
        jnp.zeros((total_rows, head_width), jnp.float32),
    )
    key_piece = lax.all_gather(key_states, "blk", axis=0, tiled=True)
    value_piece = lax.all_gather(value_states, "blk", axis=0, tiled=True)
    piece_rows = key_piece.shape[0]

    def sub_step(sub_num, inner_state):
        first = sub_num * tok_rows
        key_sub = lax.dynamic_slice_in_dim(key_piece, first, tok_rows, 0)
        value_sub = lax.dynamic_slice_in_dim(value_piece, first, tok_rows, 0)
        key_ids = first + jnp.arange(tok_rows, dtype=jnp.int32)
        owners = key_ids // tok_rows
        owner_blocks = jnp.sum(
            jnp.where(
                owners[:, None] == jnp.arange(cycle_size, dtype=jnp.int32)[None, :],
                block_order[None, :],
                0,
            ),
            axis=1,
        )
        key_pos = owner_blocks * tok_rows + key_ids % tok_rows
        return guarded_update(inner_state, key_sub, value_sub, mask_for(my_block, key_pos))

    run_max, run_sum, run_acc = lax.fori_loop(0, piece_rows // tok_rows, sub_step, start_state)
    log_sum = run_max + jnp.log(run_sum)
    out_rows = (run_acc / run_sum[:, None]).astype(jnp.bfloat16)
    attended = from_rows(out_rows)
    row_delta = jnp.sum(cot_rows.astype(jnp.float32) * out_rows.astype(jnp.float32), axis=1)

    def block_grads(q_part, cot_part, sum_part, delta_part, key_sub, value_sub, allowed):
        scores = (
            jnp.einsum("rd,kd->rk", q_part, key_sub, preferred_element_type=jnp.float32) * scaling
        )
        weights = jnp.where(allowed, jnp.exp(scores - sum_part[:, None]), 0.0)
        value_term = jnp.einsum(
            "rk,rd->kd", weights.astype(jnp.bfloat16), cot_part, preferred_element_type=jnp.float32
        )
        d_prob = jnp.einsum("rd,kd->rk", cot_part, value_sub, preferred_element_type=jnp.float32)
        d_score = (weights * (d_prob - delta_part[:, None])).astype(jnp.bfloat16)
        query_term = jnp.dot(d_score, key_sub, preferred_element_type=jnp.float32) * scaling
        key_term = (
            jnp.einsum("rk,rd->kd", d_score, q_part, preferred_element_type=jnp.float32) * scaling
        )
        return (query_term, key_term, value_term)

    def guarded_grads(q_part, cot_part, sum_part, delta_part, key_sub, value_sub, allowed):
        return block_grads(q_part, cot_part, sum_part, delta_part, key_sub, value_sub, allowed)

    zero_keys = jnp.zeros((tok_rows, head_width), jnp.float32)
    zero_queries = jnp.zeros((total_rows, head_width), jnp.float32)

    def key_step(step_num, carry_state):
        key_cur, value_cur, key_acc, value_acc, query_acc = carry_state
        source = (my_index - step_num) % cycle_size
        key_pos = block_order[source] * tok_rows + offsets
        allowed = mask_for(my_block, key_pos)
        query_term, key_term, value_term = guarded_grads(
            query_rows, cot_rows, log_sum, row_delta, key_cur, value_cur, allowed
        )
        return (
            key_cur,
            value_cur,
            key_acc + key_term,
            value_acc + value_term,
            query_acc + query_term,
        )

    def key_turn(step_num, carry_state):
        key_cur, value_cur, key_acc, value_acc, query_acc = key_step(step_num, carry_state)
        key_cur, value_cur = passed_along((key_cur, value_cur), "blk", 1)
        key_acc, value_acc = passed_along((key_acc, value_acc), "blk", 1)
        return (key_cur, value_cur, key_acc, value_acc, query_acc)

    carry_state = (key_states, value_states, zero_keys, zero_keys, zero_queries)
    carry_state = lax.fori_loop(0, cycle_size - 1, key_turn, carry_state)
    carry_state = key_step(cycle_size - 1, carry_state)
    key_acc, value_acc = passed_along((carry_state[2], carry_state[3]), "blk", 1)
    query_acc = carry_state[4]
    grad_queries = from_rows(query_acc.astype(jnp.bfloat16))
    return (attended, grad_queries, key_acc, value_acc)


def solution(mesh):
    placed = (
        P(("groups", "blk"), None),
        P(("groups", "blk"), None),
        P(("groups", "blk"), None),
        P(("groups", "blk"), None),
        P("groups", None),
        P("groups"),
    )
    return jax.shard_map(
        shards,
        mesh=mesh,
        in_specs=placed,
        out_specs=(
            P(("groups", "blk"), None),
            P(("groups", "blk"), None),
            P(("groups", "blk"), None),
            P(("groups", "blk"), None),
        ),
        check_vma=False,
    )
```

profile of v0, /device:TPU:0, one launch (start us, length us, event | category | flops | bytes accessed | tf_op | source)
XLA Modules:
  0.0 222.9 jit_solution(3966216597943441637)
XLA Ops:
  0.7 0.8 copy.83
  6.8 24.6 %all_gather.6 = bf16[2048,128]{1,0:T(8,128)(2,1)S(1)} all-gather(bf16[128,128]{1,0:T(8,128)(2,1)S(1)} %copy.83), channel_id=1, replica_groups=mesh['groups'=2,'blk'=16] {'blk'}, dimensions={0}, use_global_device_ids=true | all-gather | bytes 557056 | tf_op jit(solution)/shard_map/all_gather | solution.py:83
  31.4 18.9 %all_gather.7 = bf16[2048,128]{1,0:T(8,128)(2,1)S(1)} all-gather(bf16[128,128]{1,0:T(8,128)(2,1)S(1)} %copy.84), channel_id=1, replica_groups=mesh['groups'=2,'blk'=16] {'blk'}, dimensions={0}, use_global_device_ids=true | all-gather | bytes 557056 | tf_op jit(solution)/shard_map/all_gather | solution.py:84
  50.2 17.7 %while.47 = (s32[]{:T(128)}, f32[512]{0:T(512)S(1)}, f32[512]{0:T(512)S(1)}, f32[512,128]{1,0:T(8,128)S(1)}, s32[]{:T(128)}, /*index=5*/s32[16]{0:T(128)S(1)}, b...) while((s32[]{:T(128)}, f32[512]{0:T(512)S(1)}, ...), condition=%wide.region_4.5_spmd.clone, body=%wide.region_0.4_spmd.clone.sunk | while | flops 34965508 | bytes 1841459 | solution.py:104
  69.2 144.8 %while.48 = (s32[]{:T(128)}, bf16[128,128]{1,0:T(8,128)(2,1)S(1)}, bf16[128,128]{1,0:T(8,128)(2,1)S(1)}, f32[128,128]{1,0:T(8,128)S(1)}, f32[128,128]{1,0:T(8,12...) while((s32[]{:T(128)}, bf16[128,128]{1,0:T(8,128)(2,1)S(1)}, ...), condition=%wide.region_7.8_spmd.clone.clone, body=%wide.region_6.7_spmd.clone.clone.sunk | while | flops 85202960 | bytes 3711538 | solution.py:155
  69.7 1.5 collective-permute-start.1
  74.4 0.9 collective-permute-done
  75.7 4.2 %collective-permute-done.2 = f32[128,128]{1,0:T(8,128)S(1)} collective-permute-done((f32[128,128]{1,0:T(8,128)S(1)}, f32[128,128]{1,0:T(8,128)S(1)}, u32[]{:S(2)}, u32[]{:S(2)}) %collective-permute-start.2) | collective-permute-done | bytes 65568 | tf_op jit(solution)/shard_map/while/body/eval_jaxpr/ppermute | solution.py:12
  79.9 0.7 collective-permute-done.3
  83.6 3.1 %collective-permute-done = bf16[128,128]{1,0:T(8,128)(2,1)S(1)} collective-permute-done((bf16[128,128]{1,0:T(8,128)(2,1)S(1)}, bf16[128,128]{1,0:T(8,128)(2,1)S(1)}, u32[]{:S(2)}, u32[]{:S(2)}) %collective-permute-start) | collective-permute-done | bytes 32800 | tf_op jit(solution)/shard_map/while/body/eval_jaxpr/ppermute | solution.py:12
  87.0 2.4 %collective-permute-done.2 = f32[128,128]{1,0:T(8,128)S(1)} collective-permute-done((f32[128,128]{1,0:T(8,128)S(1)}, f32[128,128]{1,0:T(8,128)S(1)}, u32[]{:S(2)}, u32[]{:S(2)}) %collective-permute-start.2) | collective-permute-done | bytes 65568 | tf_op jit(solution)/shard_map/while/body/eval_jaxpr/ppermute | solution.py:12
  89.4 0.7 collective-permute-done.3
  93.1 3.1 %collective-permute-done = bf16[128,128]{1,0:T(8,128)(2,1)S(1)} collective-permute-done((bf16[128,128]{1,0:T(8,128)(2,1)S(1)}, bf16[128,128]{1,0:T(8,128)(2,1)S(1)}, u32[]{:S(2)}, u32[]{:S(2)}) %collective-permute-start) | collective-permute-done | bytes 32800 | tf_op jit(solution)/shard_map/while/body/eval_jaxpr/ppermute | solution.py:12
  96.5 2.4 %collective-permute-done.2 = f32[128,128]{1,0:T(8,128)S(1)} collective-permute-done((f32[128,128]{1,0:T(8,128)S(1)}, f32[128,128]{1,0:T(8,128)S(1)}, u32[]{:S(2)}, u32[]{:S(2)}) %collective-permute-start.2) | collective-permute-done | bytes 65568 | tf_op jit(solution)/shard_map/while/body/eval_jaxpr/ppermute | solution.py:12
  98.9 0.7 collective-permute-done.3
  102.6 3.1 %collective-permute-done = bf16[128,128]{1,0:T(8,128)(2,1)S(1)} collective-permute-done((bf16[128,128]{1,0:T(8,128)(2,1)S(1)}, bf16[128,128]{1,0:T(8,128)(2,1)S(1)}, u32[]{:S(2)}, u32[]{:S(2)}) %collective-permute-start) | collective-permute-done | bytes 32800 | tf_op jit(solution)/shard_map/while/body/eval_jaxpr/ppermute | solution.py:12
  106.0 2.4 %collective-permute-done.2 = f32[128,128]{1,0:T(8,128)S(1)} collective-permute-done((f32[128,128]{1,0:T(8,128)S(1)}, f32[128,128]{1,0:T(8,128)S(1)}, u32[]{:S(2)}, u32[]{:S(2)}) %collective-permute-start.2) | collective-permute-done | bytes 65568 | tf_op jit(solution)/shard_map/while/body/eval_jaxpr/ppermute | solution.py:12
  108.5 0.7 collective-permute-done.3
  112.2 3.1 %collective-permute-done = bf16[128,128]{1,0:T(8,128)(2,1)S(1)} collective-permute-done((bf16[128,128]{1,0:T(8,128)(2,1)S(1)}, bf16[128,128]{1,0:T(8,128)(2,1)S(1)}, u32[]{:S(2)}, u32[]{:S(2)}) %collective-permute-start) | collective-permute-done | bytes 32800 | tf_op jit(solution)/shard_map/while/body/eval_jaxpr/ppermute | solution.py:12
  115.6 2.4 %collective-permute-done.2 = f32[128,128]{1,0:T(8,128)S(1)} collective-permute-done((f32[128,128]{1,0:T(8,128)S(1)}, f32[128,128]{1,0:T(8,128)S(1)}, u32[]{:S(2)}, u32[]{:S(2)}) %collective-permute-start.2) | collective-permute-done | bytes 65568 | tf_op jit(solution)/shard_map/while/body/eval_jaxpr/ppermute | solution.py:12
  118.0 0.7 collective-permute-done.3
  121.7 3.1 %collective-permute-done = bf16[128,128]{1,0:T(8,128)(2,1)S(1)} collective-permute-done((bf16[128,128]{1,0:T(8,128)(2,1)S(1)}, bf16[128,128]{1,0:T(8,128)(2,1)S(1)}, u32[]{:S(2)}, u32[]{:S(2)}) %collective-permute-start) | collective-permute-done | bytes 32800 | tf_op jit(solution)/shard_map/while/body/eval_jaxpr/ppermute | solution.py:12
  125.1 2.4 %collective-permute-done.2 = f32[128,128]{1,0:T(8,128)S(1)} collective-permute-done((f32[128,128]{1,0:T(8,128)S(1)}, f32[128,128]{1,0:T(8,128)S(1)}, u32[]{:S(2)}, u32[]{:S(2)}) %collective-permute-start.2) | collective-permute-done | bytes 65568 | tf_op jit(solution)/shard_map/while/body/eval_jaxpr/ppermute | solution.py:12
  127.5 0.7 collective-permute-done.3
  131.2 3.1 %collective-permute-done = bf16[128,128]{1,0:T(8,128)(2,1)S(1)} collective-permute-done((bf16[128,128]{1,0:T(8,128)(2,1)S(1)}, bf16[128,128]{1,0:T(8,128)(2,1)S(1)}, u32[]{:S(2)}, u32[]{:S(2)}) %collective-permute-start) | collective-permute-done | bytes 32800 | tf_op jit(solution)/shard_map/while/body/eval_jaxpr/ppermute | solution.py:12
  134.6 2.4 %collective-permute-done.2 = f32[128,128]{1,0:T(8,128)S(1)} collective-permute-done((f32[128,128]{1,0:T(8,128)S(1)}, f32[128,128]{1,0:T(8,128)S(1)}, u32[]{:S(2)}, u32[]{:S(2)}) %collective-permute-start.2) | collective-permute-done | bytes 65568 | tf_op jit(solution)/shard_map/while/body/eval_jaxpr/ppermute | solution.py:12
  137.1 0.7 collective-permute-done.3
  140.8 3.1 %collective-permute-done = bf16[128,128]{1,0:T(8,128)(2,1)S(1)} collective-permute-done((bf16[128,128]{1,0:T(8,128)(2,1)S(1)}, bf16[128,128]{1,0:T(8,128)(2,1)S(1)}, u32[]{:S(2)}, u32[]{:S(2)}) %collective-permute-start) | collective-permute-done | bytes 32800 | tf_op jit(solution)/shard_map/while/body/eval_jaxpr/ppermute | solution.py:12
  144.2 2.4 %collective-permute-done.2 = f32[128,128]{1,0:T(8,128)S(1)} collective-permute-done((f32[128,128]{1,0:T(8,128)S(1)}, f32[128,128]{1,0:T(8,128)S(1)}, u32[]{:S(2)}, u32[]{:S(2)}) %collective-permute-start.2) | collective-permute-done | bytes 65568 | tf_op jit(solution)/shard_map/while/body/eval_jaxpr/ppermute | solution.py:12
  146.6 0.7 collective-permute-done.3
  150.3 3.1 %collective-permute-done = bf16[128,128]{1,0:T(8,128)(2,1)S(1)} collective-permute-done((bf16[128,128]{1,0:T(8,128)(2,1)S(1)}, bf16[128,128]{1,0:T(8,128)(2,1)S(1)}, u32[]{:S(2)}, u32[]{:S(2)}) %collective-permute-start) | collective-permute-done | bytes 32800 | tf_op jit(solution)/shard_map/while/body/eval_jaxpr/ppermute | solution.py:12
  153.7 2.4 %collective-permute-done.2 = f32[128,128]{1,0:T(8,128)S(1)} collective-permute-done((f32[128,128]{1,0:T(8,128)S(1)}, f32[128,128]{1,0:T(8,128)S(1)}, u32[]{:S(2)}, u32[]{:S(2)}) %collective-permute-start.2) | collective-permute-done | bytes 65568 | tf_op jit(solution)/shard_map/while/body/eval_jaxpr/ppermute | solution.py:12
  156.1 0.7 collective-permute-done.3
  159.8 3.1 %collective-permute-done = bf16[128,128]{1,0:T(8,128)(2,1)S(1)} collective-permute-done((bf16[128,128]{1,0:T(8,128)(2,1)S(1)}, bf16[128,128]{1,0:T(8,128)(2,1)S(1)}, u32[]{:S(2)}, u32[]{:S(2)}) %collective-permute-start) | collective-permute-done | bytes 32800 | tf_op jit(solution)/shard_map/while/body/eval_jaxpr/ppermute | solution.py:12
  163.2 2.4 %collective-permute-done.2 = f32[128,128]{1,0:T(8,128)S(1)} collective-permute-done((f32[128,128]{1,0:T(8,128)S(1)}, f32[128,128]{1,0:T(8,128)S(1)}, u32[]{:S(2)}, u32[]{:S(2)}) %collective-permute-start.2) | collective-permute-done | bytes 65568 | tf_op jit(solution)/shard_map/while/body/eval_jaxpr/ppermute | solution.py:12
  165.7 0.7 collective-permute-done.3
  169.4 3.1 %collective-permute-done = bf16[128,128]{1,0:T(8,128)(2,1)S(1)} collective-permute-done((bf16[128,128]{1,0:T(8,128)(2,1)S(1)}, bf16[128,128]{1,0:T(8,128)(2,1)S(1)}, u32[]{:S(2)}, u32[]{:S(2)}) %collective-permute-start) | collective-permute-done | bytes 32800 | tf_op jit(solution)/shard_map/while/body/eval_jaxpr/ppermute | solution.py:12
  172.8 2.4 %collective-permute-done.2 = f32[128,128]{1,0:T(8,128)S(1)} collective-permute-done((f32[128,128]{1,0:T(8,128)S(1)}, f32[128,128]{1,0:T(8,128)S(1)}, u32[]{:S(2)}, u32[]{:S(2)}) %collective-permute-start.2) | collective-permute-done | bytes 65568 | tf_op jit(solution)/shard_map/while/body/eval_jaxpr/ppermute | solution.py:12
  175.2 0.7 collective-permute-done.3
  178.9 3.1 %collective-permute-done = bf16[128,128]{1,0:T(8,128)(2,1)S(1)} collective-permute-done((bf16[128,128]{1,0:T(8,128)(2,1)S(1)}, bf16[128,128]{1,0:T(8,128)(2,1)S(1)}, u32[]{:S(2)}, u32[]{:S(2)}) %collective-permute-start) | collective-permute-done | bytes 32800 | tf_op jit(solution)/shard_map/while/body/eval_jaxpr/ppermute | solution.py:12
  182.3 2.4 %collective-permute-done.2 = f32[128,128]{1,0:T(8,128)S(1)} collective-permute-done((f32[128,128]{1,0:T(8,128)S(1)}, f32[128,128]{1,0:T(8,128)S(1)}, u32[]{:S(2)}, u32[]{:S(2)}) %collective-permute-start.2) | collective-permute-done | bytes 65568 | tf_op jit(solution)/shard_map/while/body/eval_jaxpr/ppermute | solution.py:12
  188.4 3.1 %collective-permute-done = bf16[128,128]{1,0:T(8,128)(2,1)S(1)} collective-permute-done((bf16[128,128]{1,0:T(8,128)(2,1)S(1)}, bf16[128,128]{1,0:T(8,128)(2,1)S(1)}, u32[]{:S(2)}, u32[]{:S(2)}) %collective-permute-start) | collective-permute-done | bytes 32800 | tf_op jit(solution)/shard_map/while/body/eval_jaxpr/ppermute | solution.py:12
  191.8 2.4 %collective-permute-done.2 = f32[128,128]{1,0:T(8,128)S(1)} collective-permute-done((f32[128,128]{1,0:T(8,128)S(1)}, f32[128,128]{1,0:T(8,128)S(1)}, u32[]{:S(2)}, u32[]{:S(2)}) %collective-permute-start.2) | collective-permute-done | bytes 65568 | tf_op jit(solution)/shard_map/while/body/eval_jaxpr/ppermute | solution.py:12
  197.9 3.1 %collective-permute-done = bf16[128,128]{1,0:T(8,128)(2,1)S(1)} collective-permute-done((bf16[128,128]{1,0:T(8,128)(2,1)S(1)}, bf16[128,128]{1,0:T(8,128)(2,1)S(1)}, u32[]{:S(2)}, u32[]{:S(2)}) %collective-permute-start) | collective-permute-done | bytes 32800 | tf_op jit(solution)/shard_map/while/body/eval_jaxpr/ppermute | solution.py:12
  201.4 2.4 %collective-permute-done.2 = f32[128,128]{1,0:T(8,128)S(1)} collective-permute-done((f32[128,128]{1,0:T(8,128)S(1)}, f32[128,128]{1,0:T(8,128)S(1)}, u32[]{:S(2)}, u32[]{:S(2)}) %collective-permute-start.2) | collective-permute-done | bytes 65568 | tf_op jit(solution)/shard_map/while/body/eval_jaxpr/ppermute | solution.py:12
  207.5 3.1 %collective-permute-done = bf16[128,128]{1,0:T(8,128)(2,1)S(1)} collective-permute-done((bf16[128,128]{1,0:T(8,128)(2,1)S(1)}, bf16[128,128]{1,0:T(8,128)(2,1)S(1)}, u32[]{:S(2)}, u32[]{:S(2)}) %collective-permute-start) | collective-permute-done | bytes 32800 | tf_op jit(solution)/shard_map/while/body/eval_jaxpr/ppermute | solution.py:12
  210.9 2.4 %collective-permute-done.2 = f32[128,128]{1,0:T(8,128)S(1)} collective-permute-done((f32[128,128]{1,0:T(8,128)S(1)}, f32[128,128]{1,0:T(8,128)S(1)}, u32[]{:S(2)}, u32[]{:S(2)}) %collective-permute-start.2) | collective-permute-done | bytes 65568 | tf_op jit(solution)/shard_map/while/body/eval_jaxpr/ppermute | solution.py:12
  216.7 4.2 %collective-permute-done.5 = f32[128,128]{1,0:T(8,128)S(1)} collective-permute-done((f32[128,128]{1,0:T(8,128)S(1)}, f32[128,128]{1,0:T(8,128)S(1)}, u32[]{:S(2)}, u32[]{:S(2)}) %collective-permute-start.5) | collective-permute-done | bytes 65568 | tf_op jit(solution)/shard_map/ppermute | solution.py:12
  (505 shorter events, 66.0 us)
Async XLA Ops:
  69.3 6.1 %collective-permute-start = (bf16[128,128]{1,0:T(8,128)(2,1)S(1)}, bf16[128,128]{1,0:T(8,128)(2,1)S(1)}, u32[]{:S(2)}, u32[]{:S(2)}) collective-permute-start(bf16[128,128]{1,0:T(8,128)(2,1)S(1)} %copy.67), channel_id=1, source_target_pairs={{0,1},{1,2},{2,3},{3,4},{4,5},{5,6},{6,7},{7,8},{8,9},{9,10},{10,1... | collective-permute-start | bytes 98312 | tf_op jit(solution)/shard_map/while/body/eval_jaxpr/ppermute | solution.py:12
  73.4 6.4 %collective-permute-start.2 = (f32[128,128]{1,0:T(8,128)S(1)}, f32[128,128]{1,0:T(8,128)S(1)}, u32[]{:S(2)}, u32[]{:S(2)}) collective-permute-start(f32[128,128]{1,0:T(8,128)S(1)} %fusion.122), channel_id=1, source_target_pairs={{0,1},{1,2},{2,3},{3,4},{4,5},{5,6},{6,7},{7,8},{8,9},{9,10},{10,1... | collective-permute-start | bytes 196616 | tf_op jit(solution)/shard_map/while/body/eval_jaxpr/ppermute | solution.py:12
  74.1 6.5 %collective-permute-start.3 = (f32[128,128]{1,0:T(8,128)S(1)}, f32[128,128]{1,0:T(8,128)S(1)}, u32[]{:S(2)}, u32[]{:S(2)}) collective-permute-start(f32[128,128]{1,0:T(8,128)S(1)} %convolution_add_fusion.6), channel_id=1, source_target_pairs={{0,1},{1,2},{2,3},{3,4},{4,5},{5,6},{6,7},{7,8},{8,9},{9,10},{10,1... | collective-permute-start | bytes 196616 | tf_op jit(solution)/shard_map/while/body/eval_jaxpr/ppermute | solution.py:12
  80.6 6.4 %collective-permute-start.1 = (bf16[128,128]{1,0:T(8,128)(2,1)S(1)}, bf16[128,128]{1,0:T(8,128)(2,1)S(1)}, u32[]{:S(2)}, u32[]{:S(2)}) collective-permute-start(bf16[128,128]{1,0:T(8,128)(2,1)S(1)} %copy.68), channel_id=1, source_target_pairs={{0,1},{1,2},{2,3},{3,4},{4,5},{5,6},{6,7},{7,8},{8,9},{9,10},{10,1... | collective-permute-start | bytes 98312 | tf_op jit(solution)/shard_map/while/body/eval_jaxpr/ppermute | solution.py:12
  83.0 6.4 %collective-permute-start.2 = (f32[128,128]{1,0:T(8,128)S(1)}, f32[128,128]{1,0:T(8,128)S(1)}, u32[]{:S(2)}, u32[]{:S(2)}) collective-permute-start(f32[128,128]{1,0:T(8,128)S(1)} %fusion.122), channel_id=1, source_target_pairs={{0,1},{1,2},{2,3},{3,4},{4,5},{5,6},{6,7},{7,8},{8,9},{9,10},{10,1... | collective-permute-start | bytes 196616 | tf_op jit(solution)/shard_map/while/body/eval_jaxpr/ppermute | solution.py:12
  83.3 6.8 %collective-permute-start.3 = (f32[128,128]{1,0:T(8,128)S(1)}, f32[128,128]{1,0:T(8,128)S(1)}, u32[]{:S(2)}, u32[]{:S(2)}) collective-permute-start(f32[128,128]{1,0:T(8,128)S(1)} %convolution_add_fusion.6), channel_id=1, source_target_pairs={{0,1},{1,2},{2,3},{3,4},{4,5},{5,6},{6,7},{7,8},{8,9},{9,10},{10,1... | collective-permute-start | bytes 196616 | tf_op jit(solution)/shard_map/while/body/eval_jaxpr/ppermute | solution.py:12
  90.1 6.4 %collective-permute-start.1 = (bf16[128,128]{1,0:T(8,128)(2,1)S(1)}, bf16[128,128]{1,0:T(8,128)(2,1)S(1)}, u32[]{:S(2)}, u32[]{:S(2)}) collective-permute-start(bf16[128,128]{1,0:T(8,128)(2,1)S(1)} %copy.68), channel_id=1, source_target_pairs={{0,1},{1,2},{2,3},{3,4},{4,5},{5,6},{6,7},{7,8},{8,9},{9,10},{10,1... | collective-permute-start | bytes 98312 | tf_op jit(solution)/shard_map/while/body/eval_jaxpr/ppermute | solution.py:12
  92.5 6.4 %collective-permute-start.2 = (f32[128,128]{1,0:T(8,128)S(1)}, f32[128,128]{1,0:T(8,128)S(1)}, u32[]{:S(2)}, u32[]{:S(2)}) collective-permute-start(f32[128,128]{1,0:T(8,128)S(1)} %fusion.122), channel_id=1, source_target_pairs={{0,1},{1,2},{2,3},{3,4},{4,5},{5,6},{6,7},{7,8},{8,9},{9,10},{10,1... | collective-permute-start | bytes 196616 | tf_op jit(solution)/shard_map/while/body/eval_jaxpr/ppermute | solution.py:12
  92.8 6.8 %collective-permute-start.3 = (f32[128,128]{1,0:T(8,128)S(1)}, f32[128,128]{1,0:T(8,128)S(1)}, u32[]{:S(2)}, u32[]{:S(2)}) collective-permute-start(f32[128,128]{1,0:T(8,128)S(1)} %convolution_add_fusion.6), channel_id=1, source_target_pairs={{0,1},{1,2},{2,3},{3,4},{4,5},{5,6},{6,7},{7,8},{8,9},{9,10},{10,1... | collective-permute-start | bytes 196616 | tf_op jit(solution)/shard_map/while/body/eval_jaxpr/ppermute | solution.py:12
  99.7 6.4 %collective-permute-start.1 = (bf16[128,128]{1,0:T(8,128)(2,1)S(1)}, bf16[128,128]{1,0:T(8,128)(2,1)S(1)}, u32[]{:S(2)}, u32[]{:S(2)}) collective-permute-start(bf16[128,128]{1,0:T(8,128)(2,1)S(1)} %copy.68), channel_id=1, source_target_pairs={{0,1},{1,2},{2,3},{3,4},{4,5},{5,6},{6,7},{7,8},{8,9},{9,10},{10,1... | collective-permute-start | bytes 98312 | tf_op jit(solution)/shard_map/while/body/eval_jaxpr/ppermute | solution.py:12
  102.0 6.4 %collective-permute-start.2 = (f32[128,128]{1,0:T(8,128)S(1)}, f32[128,128]{1,0:T(8,128)S(1)}, u32[]{:S(2)}, u32[]{:S(2)}) collective-permute-start(f32[128,128]{1,0:T(8,128)S(1)} %fusion.122), channel_id=1, source_target_pairs={{0,1},{1,2},{2,3},{3,4},{4,5},{5,6},{6,7},{7,8},{8,9},{9,10},{10,1... | collective-permute-start | bytes 196616 | tf_op jit(solution)/shard_map/while/body/eval_jaxpr/ppermute | solution.py:12
  102.3 6.8 %collective-permute-start.3 = (f32[128,128]{1,0:T(8,128)S(1)}, f32[128,128]{1,0:T(8,128)S(1)}, u32[]{:S(2)}, u32[]{:S(2)}) collective-permute-start(f32[128,128]{1,0:T(8,128)S(1)} %convolution_add_fusion.6), channel_id=1, source_target_pairs={{0,1},{1,2},{2,3},{3,4},{4,5},{5,6},{6,7},{7,8},{8,9},{9,10},{10,1... | collective-permute-start | bytes 196616 | tf_op jit(solution)/shard_map/while/body/eval_jaxpr/ppermute | solution.py:12
  109.2 6.4 %collective-permute-start.1 = (bf16[128,128]{1,0:T(8,128)(2,1)S(1)}, bf16[128,128]{1,0:T(8,128)(2,1)S(1)}, u32[]{:S(2)}, u32[]{:S(2)}) collective-permute-start(bf16[128,128]{1,0:T(8,128)(2,1)S(1)} %copy.68), channel_id=1, source_target_pairs={{0,1},{1,2},{2,3},{3,4},{4,5},{5,6},{6,7},{7,8},{8,9},{9,10},{10,1... | collective-permute-start | bytes 98312 | tf_op jit(solution)/shard_map/while/body/eval_jaxpr/ppermute | solution.py:12
  111.6 6.4 %collective-permute-start.2 = (f32[128,128]{1,0:T(8,128)S(1)}, f32[128,128]{1,0:T(8,128)S(1)}, u32[]{:S(2)}, u32[]{:S(2)}) collective-permute-start(f32[128,128]{1,0:T(8,128)S(1)} %fusion.122), channel_id=1, source_target_pairs={{0,1},{1,2},{2,3},{3,4},{4,5},{5,6},{6,7},{7,8},{8,9},{9,10},{10,1... | collective-permute-start | bytes 196616 | tf_op jit(solution)/shard_map/while/body/eval_jaxpr/ppermute | solution.py:12
  111.9 6.8 %collective-permute-start.3 = (f32[128,128]{1,0:T(8,128)S(1)}, f32[128,128]{1,0:T(8,128)S(1)}, u32[]{:S(2)}, u32[]{:S(2)}) collective-permute-start(f32[128,128]{1,0:T(8,128)S(1)} %convolution_add_fusion.6), channel_id=1, source_target_pairs={{0,1},{1,2},{2,3},{3,4},{4,5},{5,6},{6,7},{7,8},{8,9},{9,10},{10,1... | collective-permute-start | bytes 196616 | tf_op jit(solution)/shard_map/while/body/eval_jaxpr/ppermute | solution.py:12
  118.7 6.4 %collective-permute-start.1 = (bf16[128,128]{1,0:T(8,128)(2,1)S(1)}, bf16[128,128]{1,0:T(8,128)(2,1)S(1)}, u32[]{:S(2)}, u32[]{:S(2)}) collective-permute-start(bf16[128,128]{1,0:T(8,128)(2,1)S(1)} %copy.68), channel_id=1, source_target_pairs={{0,1},{1,2},{2,3},{3,4},{4,5},{5,6},{6,7},{7,8},{8,9},{9,10},{10,1... | collective-permute-start | bytes 98312 | tf_op jit(solution)/shard_map/while/body/eval_jaxpr/ppermute | solution.py:12
  121.1 6.4 %collective-permute-start.2 = (f32[128,128]{1,0:T(8,128)S(1)}, f32[128,128]{1,0:T(8,128)S(1)}, u32[]{:S(2)}, u32[]{:S(2)}) collective-permute-start(f32[128,128]{1,0:T(8,128)S(1)} %fusion.122), channel_id=1, source_target_pairs={{0,1},{1,2},{2,3},{3,4},{4,5},{5,6},{6,7},{7,8},{8,9},{9,10},{10,1... | collective-permute-start | bytes 196616 | tf_op jit(solution)/shard_map/while/body/eval_jaxpr/ppermute | solution.py:12
  121.4 6.8 %collective-permute-start.3 = (f32[128,128]{1,0:T(8,128)S(1)}, f32[128,128]{1,0:T(8,128)S(1)}, u32[]{:S(2)}, u32[]{:S(2)}) collective-permute-start(f32[128,128]{1,0:T(8,128)S(1)} %convolution_add_fusion.6), channel_id=1, source_target_pairs={{0,1},{1,2},{2,3},{3,4},{4,5},{5,6},{6,7},{7,8},{8,9},{9,10},{10,1... | collective-permute-start | bytes 196616 | tf_op jit(solution)/shard_map/while/body/eval_jaxpr/ppermute | solution.py:12
  128.3 6.4 %collective-permute-start.1 = (bf16[128,128]{1,0:T(8,128)(2,1)S(1)}, bf16[128,128]{1,0:T(8,128)(2,1)S(1)}, u32[]{:S(2)}, u32[]{:S(2)}) collective-permute-start(bf16[128,128]{1,0:T(8,128)(2,1)S(1)} %copy.68), channel_id=1, source_target_pairs={{0,1},{1,2},{2,3},{3,4},{4,5},{5,6},{6,7},{7,8},{8,9},{9,10},{10,1... | collective-permute-start | bytes 98312 | tf_op jit(solution)/shard_map/while/body/eval_jaxpr/ppermute | solution.py:12
  130.6 6.4 %collective-permute-start.2 = (f32[128,128]{1,0:T(8,128)S(1)}, f32[128,128]{1,0:T(8,128)S(1)}, u32[]{:S(2)}, u32[]{:S(2)}) collective-permute-start(f32[128,128]{1,0:T(8,128)S(1)} %fusion.122), channel_id=1, source_target_pairs={{0,1},{1,2},{2,3},{3,4},{4,5},{5,6},{6,7},{7,8},{8,9},{9,10},{10,1... | collective-permute-start | bytes 196616 | tf_op jit(solution)/shard_map/while/body/eval_jaxpr/ppermute | solution.py:12
  130.9 6.8 %collective-permute-start.3 = (f32[128,128]{1,0:T(8,128)S(1)}, f32[128,128]{1,0:T(8,128)S(1)}, u32[]{:S(2)}, u32[]{:S(2)}) collective-permute-start(f32[128,128]{1,0:T(8,128)S(1)} %convolution_add_fusion.6), channel_id=1, source_target_pairs={{0,1},{1,2},{2,3},{3,4},{4,5},{5,6},{6,7},{7,8},{8,9},{9,10},{10,1... | collective-permute-start | bytes 196616 | tf_op jit(solution)/shard_map/while/body/eval_jaxpr/ppermute | solution.py:12
  137.8 6.4 %collective-permute-start.1 = (bf16[128,128]{1,0:T(8,128)(2,1)S(1)}, bf16[128,128]{1,0:T(8,128)(2,1)S(1)}, u32[]{:S(2)}, u32[]{:S(2)}) collective-permute-start(bf16[128,128]{1,0:T(8,128)(2,1)S(1)} %copy.68), channel_id=1, source_target_pairs={{0,1},{1,2},{2,3},{3,4},{4,5},{5,6},{6,7},{7,8},{8,9},{9,10},{10,1... | collective-permute-start | bytes 98312 | tf_op jit(solution)/shard_map/while/body/eval_jaxpr/ppermute | solution.py:12
  140.2 6.4 %collective-permute-start.2 = (f32[128,128]{1,0:T(8,128)S(1)}, f32[128,128]{1,0:T(8,128)S(1)}, u32[]{:S(2)}, u32[]{:S(2)}) collective-permute-start(f32[128,128]{1,0:T(8,128)S(1)} %fusion.122), channel_id=1, source_target_pairs={{0,1},{1,2},{2,3},{3,4},{4,5},{5,6},{6,7},{7,8},{8,9},{9,10},{10,1... | collective-permute-start | bytes 196616 | tf_op jit(solution)/shard_map/while/body/eval_jaxpr/ppermute | solution.py:12
  140.5 6.8 %collective-permute-start.3 = (f32[128,128]{1,0:T(8,128)S(1)}, f32[128,128]{1,0:T(8,128)S(1)}, u32[]{:S(2)}, u32[]{:S(2)}) collective-permute-start(f32[128,128]{1,0:T(8,128)S(1)} %convolution_add_fusion.6), channel_id=1, source_target_pairs={{0,1},{1,2},{2,3},{3,4},{4,5},{5,6},{6,7},{7,8},{8,9},{9,10},{10,1... | collective-permute-start | bytes 196616 | tf_op jit(solution)/shard_map/while/body/eval_jaxpr/ppermute | solution.py:12
  147.3 6.4 %collective-permute-start.1 = (bf16[128,128]{1,0:T(8,128)(2,1)S(1)}, bf16[128,128]{1,0:T(8,128)(2,1)S(1)}, u32[]{:S(2)}, u32[]{:S(2)}) collective-permute-start(bf16[128,128]{1,0:T(8,128)(2,1)S(1)} %copy.68), channel_id=1, source_target_pairs={{0,1},{1,2},{2,3},{3,4},{4,5},{5,6},{6,7},{7,8},{8,9},{9,10},{10,1... | collective-permute-start | bytes 98312 | tf_op jit(solution)/shard_map/while/body/eval_jaxpr/ppermute | solution.py:12
  149.7 6.4 %collective-permute-start.2 = (f32[128,128]{1,0:T(8,128)S(1)}, f32[128,128]{1,0:T(8,128)S(1)}, u32[]{:S(2)}, u32[]{:S(2)}) collective-permute-start(f32[128,128]{1,0:T(8,128)S(1)} %fusion.122), channel_id=1, source_target_pairs={{0,1},{1,2},{2,3},{3,4},{4,5},{5,6},{6,7},{7,8},{8,9},{9,10},{10,1... | collective-permute-start | bytes 196616 | tf_op jit(solution)/shard_map/while/body/eval_jaxpr/ppermute | solution.py:12
  150.0 6.8 %collective-permute-start.3 = (f32[128,128]{1,0:T(8,128)S(1)}, f32[128,128]{1,0:T(8,128)S(1)}, u32[]{:S(2)}, u32[]{:S(2)}) collective-permute-start(f32[128,128]{1,0:T(8,128)S(1)} %convolution_add_fusion.6), channel_id=1, source_target_pairs={{0,1},{1,2},{2,3},{3,4},{4,5},{5,6},{6,7},{7,8},{8,9},{9,10},{10,1... | collective-permute-start | bytes 196616 | tf_op jit(solution)/shard_map/while/body/eval_jaxpr/ppermute | solution.py:12
  156.9 6.4 %collective-permute-start.1 = (bf16[128,128]{1,0:T(8,128)(2,1)S(1)}, bf16[128,128]{1,0:T(8,128)(2,1)S(1)}, u32[]{:S(2)}, u32[]{:S(2)}) collective-permute-start(bf16[128,128]{1,0:T(8,128)(2,1)S(1)} %copy.68), channel_id=1, source_target_pairs={{0,1},{1,2},{2,3},{3,4},{4,5},{5,6},{6,7},{7,8},{8,9},{9,10},{10,1... | collective-permute-start | bytes 98312 | tf_op jit(solution)/shard_map/while/body/eval_jaxpr/ppermute | solution.py:12
  159.2 6.4 %collective-permute-start.2 = (f32[128,128]{1,0:T(8,128)S(1)}, f32[128,128]{1,0:T(8,128)S(1)}, u32[]{:S(2)}, u32[]{:S(2)}) collective-permute-start(f32[128,128]{1,0:T(8,128)S(1)} %fusion.122), channel_id=1, source_target_pairs={{0,1},{1,2},{2,3},{3,4},{4,5},{5,6},{6,7},{7,8},{8,9},{9,10},{10,1... | collective-permute-start | bytes 196616 | tf_op jit(solution)/shard_map/while/body/eval_jaxpr/ppermute | solution.py:12
  159.5 6.8 %collective-permute-start.3 = (f32[128,128]{1,0:T(8,128)S(1)}, f32[128,128]{1,0:T(8,128)S(1)}, u32[]{:S(2)}, u32[]{:S(2)}) collective-permute-start(f32[128,128]{1,0:T(8,128)S(1)} %convolution_add_fusion.6), channel_id=1, source_target_pairs={{0,1},{1,2},{2,3},{3,4},{4,5},{5,6},{6,7},{7,8},{8,9},{9,10},{10,1... | collective-permute-start | bytes 196616 | tf_op jit(solution)/shard_map/while/body/eval_jaxpr/ppermute | solution.py:12
  166.4 6.4 %collective-permute-start.1 = (bf16[128,128]{1,0:T(8,128)(2,1)S(1)}, bf16[128,128]{1,0:T(8,128)(2,1)S(1)}, u32[]{:S(2)}, u32[]{:S(2)}) collective-permute-start(bf16[128,128]{1,0:T(8,128)(2,1)S(1)} %copy.68), channel_id=1, source_target_pairs={{0,1},{1,2},{2,3},{3,4},{4,5},{5,6},{6,7},{7,8},{8,9},{9,10},{10,1... | collective-permute-start | bytes 98312 | tf_op jit(solution)/shard_map/while/body/eval_jaxpr/ppermute | solution.py:12
  168.8 6.4 %collective-permute-start.2 = (f32[128,128]{1,0:T(8,128)S(1)}, f32[128,128]{1,0:T(8,128)S(1)}, u32[]{:S(2)}, u32[]{:S(2)}) collective-permute-start(f32[128,128]{1,0:T(8,128)S(1)} %fusion.122), channel_id=1, source_target_pairs={{0,1},{1,2},{2,3},{3,4},{4,5},{5,6},{6,7},{7,8},{8,9},{9,10},{10,1... | collective-permute-start | bytes 196616 | tf_op jit(solution)/shard_map/while/body/eval_jaxpr/ppermute | solution.py:12
  169.1 6.8 %collective-permute-start.3 = (f32[128,128]{1,0:T(8,128)S(1)}, f32[128,128]{1,0:T(8,128)S(1)}, u32[]{:S(2)}, u32[]{:S(2)}) collective-permute-start(f32[128,128]{1,0:T(8,128)S(1)} %convolution_add_fusion.6), channel_id=1, source_target_pairs={{0,1},{1,2},{2,3},{3,4},{4,5},{5,6},{6,7},{7,8},{8,9},{9,10},{10,1... | collective-permute-start | bytes 196616 | tf_op jit(solution)/shard_map/while/body/eval_jaxpr/ppermute | solution.py:12
  175.9 6.0 %collective-permute-start = (bf16[128,128]{1,0:T(8,128)(2,1)S(1)}, bf16[128,128]{1,0:T(8,128)(2,1)S(1)}, u32[]{:S(2)}, u32[]{:S(2)}) collective-permute-start(bf16[128,128]{1,0:T(8,128)(2,1)S(1)} %copy.67), channel_id=1, source_target_pairs={{0,1},{1,2},{2,3},{3,4},{4,5},{5,6},{6,7},{7,8},{8,9},{9,10},{10,1... | collective-permute-start | bytes 98312 | tf_op jit(solution)/shard_map/while/body/eval_jaxpr/ppermute | solution.py:12
  175.9 6.4 %collective-permute-start.1 = (bf16[128,128]{1,0:T(8,128)(2,1)S(1)}, bf16[128,128]{1,0:T(8,128)(2,1)S(1)}, u32[]{:S(2)}, u32[]{:S(2)}) collective-permute-start(bf16[128,128]{1,0:T(8,128)(2,1)S(1)} %copy.68), channel_id=1, source_target_pairs={{0,1},{1,2},{2,3},{3,4},{4,5},{5,6},{6,7},{7,8},{8,9},{9,10},{10,1... | collective-permute-start | bytes 98312 | tf_op jit(solution)/shard_map/while/body/eval_jaxpr/ppermute | solution.py:12
  178.3 6.4 %collective-permute-start.2 = (f32[128,128]{1,0:T(8,128)S(1)}, f32[128,128]{1,0:T(8,128)S(1)}, u32[]{:S(2)}, u32[]{:S(2)}) collective-permute-start(f32[128,128]{1,0:T(8,128)S(1)} %fusion.122), channel_id=1, source_target_pairs={{0,1},{1,2},{2,3},{3,4},{4,5},{5,6},{6,7},{7,8},{8,9},{9,10},{10,1... | collective-permute-start | bytes 196616 | tf_op jit(solution)/shard_map/while/body/eval_jaxpr/ppermute | solution.py:12
  178.6 6.8 %collective-permute-start.3 = (f32[128,128]{1,0:T(8,128)S(1)}, f32[128,128]{1,0:T(8,128)S(1)}, u32[]{:S(2)}, u32[]{:S(2)}) collective-permute-start(f32[128,128]{1,0:T(8,128)S(1)} %convolution_add_fusion.6), channel_id=1, source_target_pairs={{0,1},{1,2},{2,3},{3,4},{4,5},{5,6},{6,7},{7,8},{8,9},{9,10},{10,1... | collective-permute-start | bytes 196616 | tf_op jit(solution)/shard_map/while/body/eval_jaxpr/ppermute | solution.py:12
  185.5 6.4 %collective-permute-start.1 = (bf16[128,128]{1,0:T(8,128)(2,1)S(1)}, bf16[128,128]{1,0:T(8,128)(2,1)S(1)}, u32[]{:S(2)}, u32[]{:S(2)}) collective-permute-start(bf16[128,128]{1,0:T(8,128)(2,1)S(1)} %copy.68), channel_id=1, source_target_pairs={{0,1},{1,2},{2,3},{3,4},{4,5},{5,6},{6,7},{7,8},{8,9},{9,10},{10,1... | collective-permute-start | bytes 98312 | tf_op jit(solution)/shard_map/while/body/eval_jaxpr/ppermute | solution.py:12
  187.8 6.4 %collective-permute-start.2 = (f32[128,128]{1,0:T(8,128)S(1)}, f32[128,128]{1,0:T(8,128)S(1)}, u32[]{:S(2)}, u32[]{:S(2)}) collective-permute-start(f32[128,128]{1,0:T(8,128)S(1)} %fusion.122), channel_id=1, source_target_pairs={{0,1},{1,2},{2,3},{3,4},{4,5},{5,6},{6,7},{7,8},{8,9},{9,10},{10,1... | collective-permute-start | bytes 196616 | tf_op jit(solution)/shard_map/while/body/eval_jaxpr/ppermute | solution.py:12
  188.1 6.8 %collective-permute-start.3 = (f32[128,128]{1,0:T(8,128)S(1)}, f32[128,128]{1,0:T(8,128)S(1)}, u32[]{:S(2)}, u32[]{:S(2)}) collective-permute-start(f32[128,128]{1,0:T(8,128)S(1)} %convolution_add_fusion.6), channel_id=1, source_target_pairs={{0,1},{1,2},{2,3},{3,4},{4,5},{5,6},{6,7},{7,8},{8,9},{9,10},{10,1... | collective-permute-start | bytes 196616 | tf_op jit(solution)/shard_map/while/body/eval_jaxpr/ppermute | solution.py:12
  195.0 6.4 %collective-permute-start.1 = (bf16[128,128]{1,0:T(8,128)(2,1)S(1)}, bf16[128,128]{1,0:T(8,128)(2,1)S(1)}, u32[]{:S(2)}, u32[]{:S(2)}) collective-permute-start(bf16[128,128]{1,0:T(8,128)(2,1)S(1)} %copy.68), channel_id=1, source_target_pairs={{0,1},{1,2},{2,3},{3,4},{4,5},{5,6},{6,7},{7,8},{8,9},{9,10},{10,1... | collective-permute-start | bytes 98312 | tf_op jit(solution)/shard_map/while/body/eval_jaxpr/ppermute | solution.py:12
  197.4 6.4 %collective-permute-start.2 = (f32[128,128]{1,0:T(8,128)S(1)}, f32[128,128]{1,0:T(8,128)S(1)}, u32[]{:S(2)}, u32[]{:S(2)}) collective-permute-start(f32[128,128]{1,0:T(8,128)S(1)} %fusion.122), channel_id=1, source_target_pairs={{0,1},{1,2},{2,3},{3,4},{4,5},{5,6},{6,7},{7,8},{8,9},{9,10},{10,1... | collective-permute-start | bytes 196616 | tf_op jit(solution)/shard_map/while/body/eval_jaxpr/ppermute | solution.py:12
  197.7 6.8 %collective-permute-start.3 = (f32[128,128]{1,0:T(8,128)S(1)}, f32[128,128]{1,0:T(8,128)S(1)}, u32[]{:S(2)}, u32[]{:S(2)}) collective-permute-start(f32[128,128]{1,0:T(8,128)S(1)} %convolution_add_fusion.6), channel_id=1, source_target_pairs={{0,1},{1,2},{2,3},{3,4},{4,5},{5,6},{6,7},{7,8},{8,9},{9,10},{10,1... | collective-permute-start | bytes 196616 | tf_op jit(solution)/shard_map/while/body/eval_jaxpr/ppermute | solution.py:12
  204.5 6.4 %collective-permute-start.1 = (bf16[128,128]{1,0:T(8,128)(2,1)S(1)}, bf16[128,128]{1,0:T(8,128)(2,1)S(1)}, u32[]{:S(2)}, u32[]{:S(2)}) collective-permute-start(bf16[128,128]{1,0:T(8,128)(2,1)S(1)} %copy.68), channel_id=1, source_target_pairs={{0,1},{1,2},{2,3},{3,4},{4,5},{5,6},{6,7},{7,8},{8,9},{9,10},{10,1... | collective-permute-start | bytes 98312 | tf_op jit(solution)/shard_map/while/body/eval_jaxpr/ppermute | solution.py:12
  206.9 6.4 %collective-permute-start.2 = (f32[128,128]{1,0:T(8,128)S(1)}, f32[128,128]{1,0:T(8,128)S(1)}, u32[]{:S(2)}, u32[]{:S(2)}) collective-permute-start(f32[128,128]{1,0:T(8,128)S(1)} %fusion.122), channel_id=1, source_target_pairs={{0,1},{1,2},{2,3},{3,4},{4,5},{5,6},{6,7},{7,8},{8,9},{9,10},{10,1... | collective-permute-start | bytes 196616 | tf_op jit(solution)/shard_map/while/body/eval_jaxpr/ppermute | solution.py:12
  207.2 6.8 %collective-permute-start.3 = (f32[128,128]{1,0:T(8,128)S(1)}, f32[128,128]{1,0:T(8,128)S(1)}, u32[]{:S(2)}, u32[]{:S(2)}) collective-permute-start(f32[128,128]{1,0:T(8,128)S(1)} %convolution_add_fusion.6), channel_id=1, source_target_pairs={{0,1},{1,2},{2,3},{3,4},{4,5},{5,6},{6,7},{7,8},{8,9},{9,10},{10,1... | collective-permute-start | bytes 196616 | tf_op jit(solution)/shard_map/while/body/eval_jaxpr/ppermute | solution.py:12
  214.5 6.4 %collective-permute-start.5 = (f32[128,128]{1,0:T(8,128)S(1)}, f32[128,128]{1,0:T(8,128)S(1)}, u32[]{:S(2)}, u32[]{:S(2)}) collective-permute-start(f32[128,128]{1,0:T(8,128)S(1)} %convolution_add_fusion.2), channel_id=1, source_target_pairs={{0,1},{1,2},{2,3},{3,4},{4,5},{5,6},{6,7},{7,8},{8,9},{9,10},{10,1... | collective-permute-start | bytes 196616 | tf_op jit(solution)/shard_map/ppermute | solution.py:12
  215.0 6.7 %collective-permute-start.4 = (f32[128,128]{1,0:T(8,128)S(1)}, f32[128,128]{1,0:T(8,128)S(1)}, u32[]{:S(2)}, u32[]{:S(2)}) collective-permute-start(f32[128,128]{1,0:T(8,128)S(1)} %fusion.45), channel_id=1, source_target_pairs={{0,1},{1,2},{2,3},{3,4},{4,5},{5,6},{6,7},{7,8},{8,9},{9,10},{10,1... | collective-permute-start | bytes 196616 | tf_op jit(solution)/shard_map/ppermute | solution.py:12
  (18 other events, 109.8 us)
where the time goes:
time: 223 us
  waiting for transfers between devices  103 us (46%)
  blocking collectives  43.4 us (19%)
  matrix products  31.7 us (14%)
  local copies, waits for them, and re-layouts  17 us (8%)
  loops' own time  13 us (6%)
  other arithmetic  5.81 us (3%)
  starting transfers between devices  5 us (2%)
  between operations  4.08 us (2%)
    ppermute x62, waiting for transfers between devices, passed_along(): return lax.ppermute(value, axis, pairs)  103 us
    all_gather x1, blocking collectives, shards(): key_piece = lax.all_gather(key_states, 'blk', axis=0, tiled=True)  24.6 us
    all_gather x1, blocking collectives, shards(): value_piece = lax.all_gather(value_states, 'blk', axis=0, tiled=True)  18.9 us
    another operation x1, loops' own time, shards(): carry_state = lax.fori_loop(0, cycle_size - 1, key_turn, carry_state)  11.7 us
    dynamic_slice x16, local copies, waits for them, and re-layouts, key_step(): key_pos = block_order[source] * tok_rows + offsets  9.38 us
    dot_general x32, matrix products, mask_for(): jnp.dot(tile_rows, one_hot.T, preferred_element_type=jnp.float32) > 0.5  6.53 us
    ppermute x62, starting transfers between devices, passed_along(): return lax.ppermute(value, axis, pairs)  5 us
    dot_general x16, matrix products, softmax_update(): jnp.dot(weights.astype(jnp.bfloat16), value_sub, preferred_element_type=j...  4.83 us
  transfers between devices with their start and end apart: 62, of which 62 were waited for; matrix products, arithmetic and copies ran while one was open for 14% of the time, Pallas kernels for 0%

commit v1 on v0

--- a/solution.py
+++ b/solution.py
@@ -4,6 +4,22 @@
 from jax.sharding import PartitionSpec as P
 
 TILE = 128
+
+
+def gather_around(x, axis, dim):
+    ways, here, step = (lax.axis_size(axis), lax.axis_index(axis), x.shape[dim])
+    shape = [n * ways if d == dim else n for d, n in enumerate(x.shape)]
+    full = lax.dynamic_update_slice_in_dim(jnp.zeros(shape, x.dtype), x, here * step, axis=dim)
+    going_up = going_down = x
+    for far in range(1, ways // 2 + 1):
+        going_up = lax.ppermute(going_up, axis, [(d, (d + 1) % ways) for d in range(ways)])
+        full = lax.dynamic_update_slice_in_dim(full, going_up, (here - far) % ways * step, axis=dim)
+        if 2 * far < ways:
+            going_down = lax.ppermute(going_down, axis, [(d, (d - 1) % ways) for d in range(ways)])
+            full = lax.dynamic_update_slice_in_dim(
+                full, going_down, (here + far) % ways * step, axis=dim
+            )
+    return full
 
 
 def passed_along(value, axis, steps):
@@ -81,7 +97,7 @@
         jnp.zeros((total_rows, head_width), jnp.float32),
     )
     key_piece = lax.all_gather(key_states, "blk", axis=0, tiled=True)
-    value_piece = lax.all_gather(value_states, "blk", axis=0, tiled=True)
+    value_piece = gather_around(value_states, "blk", 0)
     piece_rows = key_piece.shape[0]
 
     def sub_step(sub_num, inner_state):

time: 223 us -> 247 us (1.11)
  starting transfers between devices: 5 us -> 35 us
  blocking collectives: 43.4 us -> 20.9 us
  waiting for transfers between devices: 103 us -> 119 us
    ppermute x0 -> x15, starting transfers between devices: none -> 32.2 us  [the longest x7 31.3 us: gather_around(): lax.ppermute(going_down, axis, [(d, (d - 1) % ways) for d in range(ways)])]
    all_gather x1 -> x0, blocking collectives: 18.9 us -> none  [shards(): value_piece = lax.all_gather(value_states, 'blk', axis=0, tiled=True)]
    ppermute x0 -> x15, waiting for transfers between devices: none -> 15.4 us  [the longest x8 15.4 us: gather_around(): lax.ppermute(going_up, axis, [(d, (d + 1) % ways) for d in range(ways)])]
    all_gather x1, blocking collectives: 24.6 us -> 20.9 us  [shards(): key_piece = lax.all_gather(key_states, 'blk', axis=0, tiled=True)]
  transfers between devices with their start and end apart: 62 -> 77, of which waited for: 62 -> 69; matrix products, arithmetic and copies ran while one was open for 14% -> 14% of each run, Pallas kernels for 0% -> 0%
where the time goes in v1:
time: 247 us
  waiting for transfers between devices  119 us (48%)
  starting transfers between devices  35 us (14%)
  matrix products  31.7 us (13%)
  blocking collectives  20.9 us (8%)
  local copies, waits for them, and re-layouts  17.3 us (7%)
  loops' own time  13.1 us (5%)
  other arithmetic  5.81 us (2%)
  between operations  4.18 us (2%)
    ppermute x62, waiting for transfers between devices, passed_along(): return lax.ppermute(value, axis, pairs)  103 us
    ppermute x7, starting transfers between devices, gather_around(): lax.ppermute(going_down, axis, [(d, (d - 1) % ways) for d in range(ways)])  31.3 us
    all_gather x1, blocking collectives, shards(): key_piece = lax.all_gather(key_states, 'blk', axis=0, tiled=True)  20.9 us
    ppermute x8, waiting for transfers between devices, gather_around(): lax.ppermute(going_up, axis, [(d, (d + 1) % ways) for d in range(ways)])  15.4 us
    another operation x1, loops' own time, shards(): carry_state = lax.fori_loop(0, cycle_size - 1, key_turn, carry_state)  11.8 us
    dynamic_slice x16, local copies, waits for them, and re-layouts, key_step(): key_pos = block_order[source] * tok_rows + offsets  9.39 us
    dot_general x32, matrix products, mask_for(): jnp.dot(tile_rows, one_hot.T, preferred_element_type=jnp.float32) > 0.5  6.53 us
  transfers between devices with their start and end apart: 77, of which 69 were waited for; matrix products, arithmetic and copies ran while one was open for 14% of the time, Pallas kernels for 0%

profile of v1, /device:TPU:0, one launch (start us, length us, event | category | flops | bytes accessed | tf_op | source)
XLA Modules:
  0.0 246.6 jit_solution(14956635678238291318)
XLA Ops:
  1.9 5.1 %collective-permute-start.5 = (bf16[128,128]{1,0:T(8,128)(2,1)S(1)}, bf16[128,128]{1,0:T(8,128)(2,1)S(1)}, u32[]{:S(2)}, u32[]{:S(2)}) collective-permute-start(bf16[128,128]{1,0:T(8,128)(2,1)S(1)} %copy.100), channel_id=1, source_target_pairs={{0,15},{1,0},{2,1},{3,2},{4,3},{5,4},{6,5},{7,6},{8,7},{9,8},{10,9... | collective-permute-start | bytes 98312 | tf_op jit(solution)/shard_map/ppermute | solution.py:18
  10.9 20.9 %all_gather.3 = bf16[2048,128]{1,0:T(8,128)(2,1)S(1)} all-gather(bf16[128,128]{1,0:T(8,128)(2,1)S(1)} %copy.99), channel_id=1, replica_groups=mesh['groups'=2,'blk'=16] {'blk'}, dimensions={0}, use_global_device_ids=true | all-gather | bytes 557056 | tf_op jit(solution)/shard_map/all_gather | solution.py:99
  34.8 4.1 %collective-permute-start.7 = (bf16[128,128]{1,0:T(8,128)(2,1)S(1)}, bf16[128,128]{1,0:T(8,128)(2,1)S(1)}, u32[]{:S(2)}, u32[]{:S(2)}) collective-permute-start(bf16[128,128]{1,0:T(8,128)(2,1)S(1)} %collective-permute-done.5), channel_id=1, source_target_pairs={{0,15},{1,0},{2,1},{3,2},{4,3},{5,4},{6,5},{7,6},{8,7},{9,8},{10,9... | collective-permute-start | bytes 98312 | tf_op jit(solution)/shard_map/ppermute | solution.py:18
  39.0 1.6 collective-permute-done.6
  40.5 4.4 %collective-permute-start.9 = (bf16[128,128]{1,0:T(8,128)(2,1)S(1)}, bf16[128,128]{1,0:T(8,128)(2,1)S(1)}, u32[]{:S(2)}, u32[]{:S(2)}) collective-permute-start(bf16[128,128]{1,0:T(8,128)(2,1)S(1)} %collective-permute-done.7), channel_id=1, source_target_pairs={{0,15},{1,0},{2,1},{3,2},{4,3},{5,4},{6,5},{7,6},{8,7},{9,8},{10,9... | collective-permute-start | bytes 98312 | tf_op jit(solution)/shard_map/ppermute | solution.py:18
  45.0 1.6 collective-permute-done.8
  46.6 4.4 %collective-permute-start.11 = (bf16[128,128]{1,0:T(8,128)(2,1)S(1)}, bf16[128,128]{1,0:T(8,128)(2,1)S(1)}, u32[]{:S(2)}, u32[]{:S(2)}) collective-permute-start(bf16[128,128]{1,0:T(8,128)(2,1)S(1)} %collective-permute-done.9), channel_id=1, source_target_pairs={{0,15},{1,0},{2,1},{3,2},{4,3},{5,4},{6,5},{7,6},{8,7},{9,8},{10,9... | collective-permute-start | bytes 98312 | tf_op jit(solution)/shard_map/ppermute | solution.py:18
  51.0 1.6 collective-permute-done.10
  52.6 4.4 %collective-permute-start.13 = (bf16[128,128]{1,0:T(8,128)(2,1)S(1)}, bf16[128,128]{1,0:T(8,128)(2,1)S(1)}, u32[]{:S(2)}, u32[]{:S(2)}) collective-permute-start(bf16[128,128]{1,0:T(8,128)(2,1)S(1)} %collective-permute-done.11), channel_id=1, source_target_pairs={{0,15},{1,0},{2,1},{3,2},{4,3},{5,4},{6,5},{7,6},{8,7},{9,8},{10,9... | collective-permute-start | bytes 98312 | tf_op jit(solution)/shard_map/ppermute | solution.py:18
  57.1 1.6 collective-permute-done.12
  58.6 4.4 %collective-permute-start.15 = (bf16[128,128]{1,0:T(8,128)(2,1)S(1)}, bf16[128,128]{1,0:T(8,128)(2,1)S(1)}, u32[]{:S(2)}, u32[]{:S(2)}) collective-permute-start(bf16[128,128]{1,0:T(8,128)(2,1)S(1)} %collective-permute-done.13), channel_id=1, source_target_pairs={{0,15},{1,0},{2,1},{3,2},{4,3},{5,4},{6,5},{7,6},{8,7},{9,8},{10,9... | collective-permute-start | bytes 98312 | tf_op jit(solution)/shard_map/ppermute | solution.py:18
  63.1 1.6 collective-permute-done.14
  64.7 4.4 %collective-permute-start.17 = (bf16[128,128]{1,0:T(8,128)(2,1)S(1)}, bf16[128,128]{1,0:T(8,128)(2,1)S(1)}, u32[]{:S(2)}, u32[]{:S(2)}) collective-permute-start(bf16[128,128]{1,0:T(8,128)(2,1)S(1)} %collective-permute-done.15), channel_id=1, source_target_pairs={{0,15},{1,0},{2,1},{3,2},{4,3},{5,4},{6,5},{7,6},{8,7},{9,8},{10,9... | collective-permute-start | bytes 98312 | tf_op jit(solution)/shard_map/ppermute | solution.py:18
  69.1 1.6 collective-permute-done.16
  70.8 6.0 %collective-permute-done.18 = bf16[128,128]{1,0:T(8,128)(2,1)S(1)} collective-permute-done((bf16[128,128]{1,0:T(8,128)(2,1)S(1)}, bf16[128,128]{1,0:T(8,128)(2,1)S(1)}, u32[]{:S(2)}, u32[]{:S(2)}) %collective-permute-start.18) | collective-permute-done | bytes 32800 | tf_op jit(solution)/shard_map/ppermute | solution.py:15
  76.8 17.6 %while.47 = (s32[]{:T(128)}, f32[512]{0:T(512)S(1)}, f32[512]{0:T(512)S(1)}, f32[512,128]{1,0:T(8,128)S(1)}, s32[]{:T(128)}, /*index=5*/s32[16]{0:T(128)S(1)}, b...) while((s32[]{:T(128)}, f32[512]{0:T(512)S(1)}, ...), condition=%wide.region_4.5_spmd.clone, body=%wide.region_0.4_spmd.clone.sunk | while | flops 34965508 | bytes 1841459 | solution.py:120
  94.7 143.1 %while.48 = (s32[]{:T(128)}, bf16[128,128]{1,0:T(8,128)(2,1)S(1)}, bf16[128,128]{1,0:T(8,128)(2,1)S(1)}, f32[128,128]{1,0:T(8,128)S(1)}, f32[128,128]{1,0:T(8,12...) while((s32[]{:T(128)}, bf16[128,128]{1,0:T(8,128)(2,1)S(1)}, ...), condition=%wide.region_7.8_spmd.clone.clone, body=%wide.region_6.7_spmd.clone.clone.sunk | while | flops 85202960 | bytes 3711538 | solution.py:171
  97.7 3.0 %collective-permute-done = bf16[128,128]{1,0:T(8,128)(2,1)S(1)} collective-permute-done((bf16[128,128]{1,0:T(8,128)(2,1)S(1)}, bf16[128,128]{1,0:T(8,128)(2,1)S(1)}, u32[]{:S(2)}, u32[]{:S(2)}) %collective-permute-start) | collective-permute-done | bytes 32800 | tf_op jit(solution)/shard_map/while/body/eval_jaxpr/ppermute | solution.py:28
  101.1 2.5 collective-permute-done.2
  107.3 3.1 %collective-permute-done = bf16[128,128]{1,0:T(8,128)(2,1)S(1)} collective-permute-done((bf16[128,128]{1,0:T(8,128)(2,1)S(1)}, bf16[128,128]{1,0:T(8,128)(2,1)S(1)}, u32[]{:S(2)}, u32[]{:S(2)}) %collective-permute-start) | collective-permute-done | bytes 32800 | tf_op jit(solution)/shard_map/while/body/eval_jaxpr/ppermute | solution.py:28
  110.7 2.4 collective-permute-done.2
  116.8 3.1 %collective-permute-done = bf16[128,128]{1,0:T(8,128)(2,1)S(1)} collective-permute-done((bf16[128,128]{1,0:T(8,128)(2,1)S(1)}, bf16[128,128]{1,0:T(8,128)(2,1)S(1)}, u32[]{:S(2)}, u32[]{:S(2)}) %collective-permute-start) | collective-permute-done | bytes 32800 | tf_op jit(solution)/shard_map/while/body/eval_jaxpr/ppermute | solution.py:28
  120.2 2.4 collective-permute-done.2
  126.3 3.1 %collective-permute-done = bf16[128,128]{1,0:T(8,128)(2,1)S(1)} collective-permute-done((bf16[128,128]{1,0:T(8,128)(2,1)S(1)}, bf16[128,128]{1,0:T(8,128)(2,1)S(1)}, u32[]{:S(2)}, u32[]{:S(2)}) %collective-permute-start) | collective-permute-done | bytes 32800 | tf_op jit(solution)/shard_map/while/body/eval_jaxpr/ppermute | solution.py:28
  129.8 2.4 collective-permute-done.2
  135.9 3.1 %collective-permute-done = bf16[128,128]{1,0:T(8,128)(2,1)S(1)} collective-permute-done((bf16[128,128]{1,0:T(8,128)(2,1)S(1)}, bf16[128,128]{1,0:T(8,128)(2,1)S(1)}, u32[]{:S(2)}, u32[]{:S(2)}) %collective-permute-start) | collective-permute-done | bytes 32800 | tf_op jit(solution)/shard_map/while/body/eval_jaxpr/ppermute | solution.py:28
  139.3 2.4 collective-permute-done.2
  145.4 3.1 %collective-permute-done = bf16[128,128]{1,0:T(8,128)(2,1)S(1)} collective-permute-done((bf16[128,128]{1,0:T(8,128)(2,1)S(1)}, bf16[128,128]{1,0:T(8,128)(2,1)S(1)}, u32[]{:S(2)}, u32[]{:S(2)}) %collective-permute-start) | collective-permute-done | bytes 32800 | tf_op jit(solution)/shard_map/while/body/eval_jaxpr/ppermute | solution.py:28
  148.8 2.4 collective-permute-done.2
  154.9 3.1 %collective-permute-done = bf16[128,128]{1,0:T(8,128)(2,1)S(1)} collective-permute-done((bf16[128,128]{1,0:T(8,128)(2,1)S(1)}, bf16[128,128]{1,0:T(8,128)(2,1)S(1)}, u32[]{:S(2)}, u32[]{:S(2)}) %collective-permute-start) | collective-permute-done | bytes 32800 | tf_op jit(solution)/shard_map/while/body/eval_jaxpr/ppermute | solution.py:28
  158.4 2.4 collective-permute-done.2
  164.5 3.1 %collective-permute-done = bf16[128,128]{1,0:T(8,128)(2,1)S(1)} collective-permute-done((bf16[128,128]{1,0:T(8,128)(2,1)S(1)}, bf16[128,128]{1,0:T(8,128)(2,1)S(1)}, u32[]{:S(2)}, u32[]{:S(2)}) %collective-permute-start) | collective-permute-done | bytes 32800 | tf_op jit(solution)/shard_map/while/body/eval_jaxpr/ppermute | solution.py:28
  167.9 2.4 collective-permute-done.2
  174.0 3.1 %collective-permute-done = bf16[128,128]{1,0:T(8,128)(2,1)S(1)} collective-permute-done((bf16[128,128]{1,0:T(8,128)(2,1)S(1)}, bf16[128,128]{1,0:T(8,128)(2,1)S(1)}, u32[]{:S(2)}, u32[]{:S(2)}) %collective-permute-start) | collective-permute-done | bytes 32800 | tf_op jit(solution)/shard_map/while/body/eval_jaxpr/ppermute | solution.py:28
  177.4 2.4 collective-permute-done.2
  183.5 3.1 %collective-permute-done = bf16[128,128]{1,0:T(8,128)(2,1)S(1)} collective-permute-done((bf16[128,128]{1,0:T(8,128)(2,1)S(1)}, bf16[128,128]{1,0:T(8,128)(2,1)S(1)}, u32[]{:S(2)}, u32[]{:S(2)}) %collective-permute-start) | collective-permute-done | bytes 32800 | tf_op jit(solution)/shard_map/while/body/eval_jaxpr/ppermute | solution.py:28
  186.9 2.4 collective-permute-done.2
  193.1 3.1 %collective-permute-done = bf16[128,128]{1,0:T(8,128)(2,1)S(1)} collective-permute-done((bf16[128,128]{1,0:T(8,128)(2,1)S(1)}, bf16[128,128]{1,0:T(8,128)(2,1)S(1)}, u32[]{:S(2)}, u32[]{:S(2)}) %collective-permute-start) | collective-permute-done | bytes 32800 | tf_op jit(solution)/shard_map/while/body/eval_jaxpr/ppermute | solution.py:28
  196.5 2.4 collective-permute-done.2
  202.6 3.1 %collective-permute-done = bf16[128,128]{1,0:T(8,128)(2,1)S(1)} collective-permute-done((bf16[128,128]{1,0:T(8,128)(2,1)S(1)}, bf16[128,128]{1,0:T(8,128)(2,1)S(1)}, u32[]{:S(2)}, u32[]{:S(2)}) %collective-permute-start) | collective-permute-done | bytes 32800 | tf_op jit(solution)/shard_map/while/body/eval_jaxpr/ppermute | solution.py:28
  206.0 2.4 collective-permute-done.2
  212.1 3.1 %collective-permute-done = bf16[128,128]{1,0:T(8,128)(2,1)S(1)} collective-permute-done((bf16[128,128]{1,0:T(8,128)(2,1)S(1)}, bf16[128,128]{1,0:T(8,128)(2,1)S(1)}, u32[]{:S(2)}, u32[]{:S(2)}) %collective-permute-start) | collective-permute-done | bytes 32800 | tf_op jit(solution)/shard_map/while/body/eval_jaxpr/ppermute | solution.py:28
  215.5 2.4 collective-permute-done.2
  221.7 3.1 %collective-permute-done = bf16[128,128]{1,0:T(8,128)(2,1)S(1)} collective-permute-done((bf16[128,128]{1,0:T(8,128)(2,1)S(1)}, bf16[128,128]{1,0:T(8,128)(2,1)S(1)}, u32[]{:S(2)}, u32[]{:S(2)}) %collective-permute-start) | collective-permute-done | bytes 32800 | tf_op jit(solution)/shard_map/while/body/eval_jaxpr/ppermute | solution.py:28
  225.1 2.4 collective-permute-done.2
  231.2 3.1 %collective-permute-done = bf16[128,128]{1,0:T(8,128)(2,1)S(1)} collective-permute-done((bf16[128,128]{1,0:T(8,128)(2,1)S(1)}, bf16[128,128]{1,0:T(8,128)(2,1)S(1)}, u32[]{:S(2)}, u32[]{:S(2)}) %collective-permute-start) | collective-permute-done | bytes 32800 | tf_op jit(solution)/shard_map/while/body/eval_jaxpr/ppermute | solution.py:28
  234.6 2.4 collective-permute-done.2
  240.4 4.2 %collective-permute-done.20 = f32[128,128]{1,0:T(8,128)S(1)} collective-permute-done((f32[128,128]{1,0:T(8,128)S(1)}, f32[128,128]{1,0:T(8,128)S(1)}, u32[]{:S(2)}, u32[]{:S(2)}) %collective-permute-start.20) | collective-permute-done | bytes 65568 | tf_op jit(solution)/shard_map/ppermute | solution.py:28
  (551 shorter events, 74.9 us)
Async XLA Ops:
  1.5 33.0 %collective-permute-start.4 = (bf16[128,128]{1,0:T(8,128)(2,1)S(1)}, bf16[128,128]{1,0:T(8,128)(2,1)S(1)}, u32[]{:S(2)}, u32[]{:S(2)}) collective-permute-start(bf16[128,128]{1,0:T(8,128)(2,1)S(1)} %copy.100), channel_id=1, source_target_pairs={{0,1},{1,2},{2,3},{3,4},{4,5},{5,6},{6,7},{7,8},{8,9},{9,10},{10,1... | collective-permute-start | bytes 98312 | tf_op jit(solution)/shard_map/ppermute | solution.py:15
  1.9 32.9 %collective-permute-start.5 = (bf16[128,128]{1,0:T(8,128)(2,1)S(1)}, bf16[128,128]{1,0:T(8,128)(2,1)S(1)}, u32[]{:S(2)}, u32[]{:S(2)}) collective-permute-start(bf16[128,128]{1,0:T(8,128)(2,1)S(1)} %copy.100), channel_id=1, source_target_pairs={{0,15},{1,0},{2,1},{3,2},{4,3},{5,4},{6,5},{7,6},{8,7},{9,8},{10,9... | collective-permute-start | bytes 98312 | tf_op jit(solution)/shard_map/ppermute | solution.py:18
  97.2 6.4 %collective-permute-start.2 = (f32[128,128]{1,0:T(8,128)S(1)}, f32[128,128]{1,0:T(8,128)S(1)}, u32[]{:S(2)}, u32[]{:S(2)}) collective-permute-start(f32[128,128]{1,0:T(8,128)S(1)} %fusion.123), channel_id=1, source_target_pairs={{0,1},{1,2},{2,3},{3,4},{4,5},{5,6},{6,7},{7,8},{8,9},{9,10},{10,1... | collective-permute-start | bytes 196616 | tf_op jit(solution)/shard_map/while/body/eval_jaxpr/ppermute | solution.py:28
  97.5 6.8 %collective-permute-start.3 = (f32[128,128]{1,0:T(8,128)S(1)}, f32[128,128]{1,0:T(8,128)S(1)}, u32[]{:S(2)}, u32[]{:S(2)}) collective-permute-start(f32[128,128]{1,0:T(8,128)S(1)} %convolution_add_fusion.6), channel_id=1, source_target_pairs={{0,1},{1,2},{2,3},{3,4},{4,5},{5,6},{6,7},{7,8},{8,9},{9,10},{10,1... | collective-permute-start | bytes 196616 | tf_op jit(solution)/shard_map/while/body/eval_jaxpr/ppermute | solution.py:28
  104.3 6.4 %collective-permute-start.1 = (bf16[128,128]{1,0:T(8,128)(2,1)S(1)}, bf16[128,128]{1,0:T(8,128)(2,1)S(1)}, u32[]{:S(2)}, u32[]{:S(2)}) collective-permute-start(bf16[128,128]{1,0:T(8,128)(2,1)S(1)} %copy.84), channel_id=1, source_target_pairs={{0,1},{1,2},{2,3},{3,4},{4,5},{5,6},{6,7},{7,8},{8,9},{9,10},{10,1... | collective-permute-start | bytes 98312 | tf_op jit(solution)/shard_map/while/body/eval_jaxpr/ppermute | solution.py:28
  106.7 6.4 %collective-permute-start.2 = (f32[128,128]{1,0:T(8,128)S(1)}, f32[128,128]{1,0:T(8,128)S(1)}, u32[]{:S(2)}, u32[]{:S(2)}) collective-permute-start(f32[128,128]{1,0:T(8,128)S(1)} %fusion.123), channel_id=1, source_target_pairs={{0,1},{1,2},{2,3},{3,4},{4,5},{5,6},{6,7},{7,8},{8,9},{9,10},{10,1... | collective-permute-start | bytes 196616 | tf_op jit(solution)/shard_map/while/body/eval_jaxpr/ppermute | solution.py:28
  107.0 6.8 %collective-permute-start.3 = (f32[128,128]{1,0:T(8,128)S(1)}, f32[128,128]{1,0:T(8,128)S(1)}, u32[]{:S(2)}, u32[]{:S(2)}) collective-permute-start(f32[128,128]{1,0:T(8,128)S(1)} %convolution_add_fusion.6), channel_id=1, source_target_pairs={{0,1},{1,2},{2,3},{3,4},{4,5},{5,6},{6,7},{7,8},{8,9},{9,10},{10,1... | collective-permute-start | bytes 196616 | tf_op jit(solution)/shard_map/while/body/eval_jaxpr/ppermute | solution.py:28
  113.8 6.4 %collective-permute-start.1 = (bf16[128,128]{1,0:T(8,128)(2,1)S(1)}, bf16[128,128]{1,0:T(8,128)(2,1)S(1)}, u32[]{:S(2)}, u32[]{:S(2)}) collective-permute-start(bf16[128,128]{1,0:T(8,128)(2,1)S(1)} %copy.84), channel_id=1, source_target_pairs={{0,1},{1,2},{2,3},{3,4},{4,5},{5,6},{6,7},{7,8},{8,9},{9,10},{10,1... | collective-permute-start | bytes 98312 | tf_op jit(solution)/shard_map/while/body/eval_jaxpr/ppermute | solution.py:28
  116.2 6.4 %collective-permute-start.2 = (f32[128,128]{1,0:T(8,128)S(1)}, f32[128,128]{1,0:T(8,128)S(1)}, u32[]{:S(2)}, u32[]{:S(2)}) collective-permute-start(f32[128,128]{1,0:T(8,128)S(1)} %fusion.123), channel_id=1, source_target_pairs={{0,1},{1,2},{2,3},{3,4},{4,5},{5,6},{6,7},{7,8},{8,9},{9,10},{10,1... | collective-permute-start | bytes 196616 | tf_op jit(solution)/shard_map/while/body/eval_jaxpr/ppermute | solution.py:28
  116.5 6.8 %collective-permute-start.3 = (f32[128,128]{1,0:T(8,128)S(1)}, f32[128,128]{1,0:T(8,128)S(1)}, u32[]{:S(2)}, u32[]{:S(2)}) collective-permute-start(f32[128,128]{1,0:T(8,128)S(1)} %convolution_add_fusion.6), channel_id=1, source_target_pairs={{0,1},{1,2},{2,3},{3,4},{4,5},{5,6},{6,7},{7,8},{8,9},{9,10},{10,1... | collective-permute-start | bytes 196616 | tf_op jit(solution)/shard_map/while/body/eval_jaxpr/ppermute | solution.py:28
  123.4 6.4 %collective-permute-start.1 = (bf16[128,128]{1,0:T(8,128)(2,1)S(1)}, bf16[128,128]{1,0:T(8,128)(2,1)S(1)}, u32[]{:S(2)}, u32[]{:S(2)}) collective-permute-start(bf16[128,128]{1,0:T(8,128)(2,1)S(1)} %copy.84), channel_id=1, source_target_pairs={{0,1},{1,2},{2,3},{3,4},{4,5},{5,6},{6,7},{7,8},{8,9},{9,10},{10,1... | collective-permute-start | bytes 98312 | tf_op jit(solution)/shard_map/while/body/eval_jaxpr/ppermute | solution.py:28
  125.8 6.4 %collective-permute-start.2 = (f32[128,128]{1,0:T(8,128)S(1)}, f32[128,128]{1,0:T(8,128)S(1)}, u32[]{:S(2)}, u32[]{:S(2)}) collective-permute-start(f32[128,128]{1,0:T(8,128)S(1)} %fusion.123), channel_id=1, source_target_pairs={{0,1},{1,2},{2,3},{3,4},{4,5},{5,6},{6,7},{7,8},{8,9},{9,10},{10,1... | collective-permute-start | bytes 196616 | tf_op jit(solution)/shard_map/while/body/eval_jaxpr/ppermute | solution.py:28
  126.1 6.8 %collective-permute-start.3 = (f32[128,128]{1,0:T(8,128)S(1)}, f32[128,128]{1,0:T(8,128)S(1)}, u32[]{:S(2)}, u32[]{:S(2)}) collective-permute-start(f32[128,128]{1,0:T(8,128)S(1)} %convolution_add_fusion.6), channel_id=1, source_target_pairs={{0,1},{1,2},{2,3},{3,4},{4,5},{5,6},{6,7},{7,8},{8,9},{9,10},{10,1... | collective-permute-start | bytes 196616 | tf_op jit(solution)/shard_map/while/body/eval_jaxpr/ppermute | solution.py:28
  132.9 6.4 %collective-permute-start.1 = (bf16[128,128]{1,0:T(8,128)(2,1)S(1)}, bf16[128,128]{1,0:T(8,128)(2,1)S(1)}, u32[]{:S(2)}, u32[]{:S(2)}) collective-permute-start(bf16[128,128]{1,0:T(8,128)(2,1)S(1)} %copy.84), channel_id=1, source_target_pairs={{0,1},{1,2},{2,3},{3,4},{4,5},{5,6},{6,7},{7,8},{8,9},{9,10},{10,1... | collective-permute-start | bytes 98312 | tf_op jit(solution)/shard_map/while/body/eval_jaxpr/ppermute | solution.py:28
  135.3 6.4 %collective-permute-start.2 = (f32[128,128]{1,0:T(8,128)S(1)}, f32[128,128]{1,0:T(8,128)S(1)}, u32[]{:S(2)}, u32[]{:S(2)}) collective-permute-start(f32[128,128]{1,0:T(8,128)S(1)} %fusion.123), channel_id=1, source_target_pairs={{0,1},{1,2},{2,3},{3,4},{4,5},{5,6},{6,7},{7,8},{8,9},{9,10},{10,1... | collective-permute-start | bytes 196616 | tf_op jit(solution)/shard_map/while/body/eval_jaxpr/ppermute | solution.py:28
  135.6 6.8 %collective-permute-start.3 = (f32[128,128]{1,0:T(8,128)S(1)}, f32[128,128]{1,0:T(8,128)S(1)}, u32[]{:S(2)}, u32[]{:S(2)}) collective-permute-start(f32[128,128]{1,0:T(8,128)S(1)} %convolution_add_fusion.6), channel_id=1, source_target_pairs={{0,1},{1,2},{2,3},{3,4},{4,5},{5,6},{6,7},{7,8},{8,9},{9,10},{10,1... | collective-permute-start | bytes 196616 | tf_op jit(solution)/shard_map/while/body/eval_jaxpr/ppermute | solution.py:28
  142.4 6.4 %collective-permute-start.1 = (bf16[128,128]{1,0:T(8,128)(2,1)S(1)}, bf16[128,128]{1,0:T(8,128)(2,1)S(1)}, u32[]{:S(2)}, u32[]{:S(2)}) collective-permute-start(bf16[128,128]{1,0:T(8,128)(2,1)S(1)} %copy.84), channel_id=1, source_target_pairs={{0,1},{1,2},{2,3},{3,4},{4,5},{5,6},{6,7},{7,8},{8,9},{9,10},{10,1... | collective-permute-start | bytes 98312 | tf_op jit(solution)/shard_map/while/body/eval_jaxpr/ppermute | solution.py:28
  144.8 6.4 %collective-permute-start.2 = (f32[128,128]{1,0:T(8,128)S(1)}, f32[128,128]{1,0:T(8,128)S(1)}, u32[]{:S(2)}, u32[]{:S(2)}) collective-permute-start(f32[128,128]{1,0:T(8,128)S(1)} %fusion.123), channel_id=1, source_target_pairs={{0,1},{1,2},{2,3},{3,4},{4,5},{5,6},{6,7},{7,8},{8,9},{9,10},{10,1... | collective-permute-start | bytes 196616 | tf_op jit(solution)/shard_map/while/body/eval_jaxpr/ppermute | solution.py:28
  145.1 6.8 %collective-permute-start.3 = (f32[128,128]{1,0:T(8,128)S(1)}, f32[128,128]{1,0:T(8,128)S(1)}, u32[]{:S(2)}, u32[]{:S(2)}) collective-permute-start(f32[128,128]{1,0:T(8,128)S(1)} %convolution_add_fusion.6), channel_id=1, source_target_pairs={{0,1},{1,2},{2,3},{3,4},{4,5},{5,6},{6,7},{7,8},{8,9},{9,10},{10,1... | collective-permute-start | bytes 196616 | tf_op jit(solution)/shard_map/while/body/eval_jaxpr/ppermute | solution.py:28
  152.0 6.4 %collective-permute-start.1 = (bf16[128,128]{1,0:T(8,128)(2,1)S(1)}, bf16[128,128]{1,0:T(8,128)(2,1)S(1)}, u32[]{:S(2)}, u32[]{:S(2)}) collective-permute-start(bf16[128,128]{1,0:T(8,128)(2,1)S(1)} %copy.84), channel_id=1, source_target_pairs={{0,1},{1,2},{2,3},{3,4},{4,5},{5,6},{6,7},{7,8},{8,9},{9,10},{10,1... | collective-permute-start | bytes 98312 | tf_op jit(solution)/shard_map/while/body/eval_jaxpr/ppermute | solution.py:28
  154.3 6.4 %collective-permute-start.2 = (f32[128,128]{1,0:T(8,128)S(1)}, f32[128,128]{1,0:T(8,128)S(1)}, u32[]{:S(2)}, u32[]{:S(2)}) collective-permute-start(f32[128,128]{1,0:T(8,128)S(1)} %fusion.123), channel_id=1, source_target_pairs={{0,1},{1,2},{2,3},{3,4},{4,5},{5,6},{6,7},{7,8},{8,9},{9,10},{10,1... | collective-permute-start | bytes 196616 | tf_op jit(solution)/shard_map/while/body/eval_jaxpr/ppermute | solution.py:28
  154.7 6.8 %collective-permute-start.3 = (f32[128,128]{1,0:T(8,128)S(1)}, f32[128,128]{1,0:T(8,128)S(1)}, u32[]{:S(2)}, u32[]{:S(2)}) collective-permute-start(f32[128,128]{1,0:T(8,128)S(1)} %convolution_add_fusion.6), channel_id=1, source_target_pairs={{0,1},{1,2},{2,3},{3,4},{4,5},{5,6},{6,7},{7,8},{8,9},{9,10},{10,1... | collective-permute-start | bytes 196616 | tf_op jit(solution)/shard_map/while/body/eval_jaxpr/ppermute | solution.py:28
  161.5 6.4 %collective-permute-start.1 = (bf16[128,128]{1,0:T(8,128)(2,1)S(1)}, bf16[128,128]{1,0:T(8,128)(2,1)S(1)}, u32[]{:S(2)}, u32[]{:S(2)}) collective-permute-start(bf16[128,128]{1,0:T(8,128)(2,1)S(1)} %copy.84), channel_id=1, source_target_pairs={{0,1},{1,2},{2,3},{3,4},{4,5},{5,6},{6,7},{7,8},{8,9},{9,10},{10,1... | collective-permute-start | bytes 98312 | tf_op jit(solution)/shard_map/while/body/eval_jaxpr/ppermute | solution.py:28
  163.9 6.4 %collective-permute-start.2 = (f32[128,128]{1,0:T(8,128)S(1)}, f32[128,128]{1,0:T(8,128)S(1)}, u32[]{:S(2)}, u32[]{:S(2)}) collective-permute-start(f32[128,128]{1,0:T(8,128)S(1)} %fusion.123), channel_id=1, source_target_pairs={{0,1},{1,2},{2,3},{3,4},{4,5},{5,6},{6,7},{7,8},{8,9},{9,10},{10,1... | collective-permute-start | bytes 196616 | tf_op jit(solution)/shard_map/while/body/eval_jaxpr/ppermute | solution.py:28
  164.2 6.8 %collective-permute-start.3 = (f32[128,128]{1,0:T(8,128)S(1)}, f32[128,128]{1,0:T(8,128)S(1)}, u32[]{:S(2)}, u32[]{:S(2)}) collective-permute-start(f32[128,128]{1,0:T(8,128)S(1)} %convolution_add_fusion.6), channel_id=1, source_target_pairs={{0,1},{1,2},{2,3},{3,4},{4,5},{5,6},{6,7},{7,8},{8,9},{9,10},{10,1... | collective-permute-start | bytes 196616 | tf_op jit(solution)/shard_map/while/body/eval_jaxpr/ppermute | solution.py:28
  171.0 6.4 %collective-permute-start.1 = (bf16[128,128]{1,0:T(8,128)(2,1)S(1)}, bf16[128,128]{1,0:T(8,128)(2,1)S(1)}, u32[]{:S(2)}, u32[]{:S(2)}) collective-permute-start(bf16[128,128]{1,0:T(8,128)(2,1)S(1)} %copy.84), channel_id=1, source_target_pairs={{0,1},{1,2},{2,3},{3,4},{4,5},{5,6},{6,7},{7,8},{8,9},{9,10},{10,1... | collective-permute-start | bytes 98312 | tf_op jit(solution)/shard_map/while/body/eval_jaxpr/ppermute | solution.py:28
  173.4 6.4 %collective-permute-start.2 = (f32[128,128]{1,0:T(8,128)S(1)}, f32[128,128]{1,0:T(8,128)S(1)}, u32[]{:S(2)}, u32[]{:S(2)}) collective-permute-start(f32[128,128]{1,0:T(8,128)S(1)} %fusion.123), channel_id=1, source_target_pairs={{0,1},{1,2},{2,3},{3,4},{4,5},{5,6},{6,7},{7,8},{8,9},{9,10},{10,1... | collective-permute-start | bytes 196616 | tf_op jit(solution)/shard_map/while/body/eval_jaxpr/ppermute | solution.py:28
  173.7 6.8 %collective-permute-start.3 = (f32[128,128]{1,0:T(8,128)S(1)}, f32[128,128]{1,0:T(8,128)S(1)}, u32[]{:S(2)}, u32[]{:S(2)}) collective-permute-start(f32[128,128]{1,0:T(8,128)S(1)} %convolution_add_fusion.6), channel_id=1, source_target_pairs={{0,1},{1,2},{2,3},{3,4},{4,5},{5,6},{6,7},{7,8},{8,9},{9,10},{10,1... | collective-permute-start | bytes 196616 | tf_op jit(solution)/shard_map/while/body/eval_jaxpr/ppermute | solution.py:28
  180.6 6.4 %collective-permute-start.1 = (bf16[128,128]{1,0:T(8,128)(2,1)S(1)}, bf16[128,128]{1,0:T(8,128)(2,1)S(1)}, u32[]{:S(2)}, u32[]{:S(2)}) collective-permute-start(bf16[128,128]{1,0:T(8,128)(2,1)S(1)} %copy.84), channel_id=1, source_target_pairs={{0,1},{1,2},{2,3},{3,4},{4,5},{5,6},{6,7},{7,8},{8,9},{9,10},{10,1... | collective-permute-start | bytes 98312 | tf_op jit(solution)/shard_map/while/body/eval_jaxpr/ppermute | solution.py:28
  182.9 6.4 %collective-permute-start.2 = (f32[128,128]{1,0:T(8,128)S(1)}, f32[128,128]{1,0:T(8,128)S(1)}, u32[]{:S(2)}, u32[]{:S(2)}) collective-permute-start(f32[128,128]{1,0:T(8,128)S(1)} %fusion.123), channel_id=1, source_target_pairs={{0,1},{1,2},{2,3},{3,4},{4,5},{5,6},{6,7},{7,8},{8,9},{9,10},{10,1... | collective-permute-start | bytes 196616 | tf_op jit(solution)/shard_map/while/body/eval_jaxpr/ppermute | solution.py:28
  183.2 6.8 %collective-permute-start.3 = (f32[128,128]{1,0:T(8,128)S(1)}, f32[128,128]{1,0:T(8,128)S(1)}, u32[]{:S(2)}, u32[]{:S(2)}) collective-permute-start(f32[128,128]{1,0:T(8,128)S(1)} %convolution_add_fusion.6), channel_id=1, source_target_pairs={{0,1},{1,2},{2,3},{3,4},{4,5},{5,6},{6,7},{7,8},{8,9},{9,10},{10,1... | collective-permute-start | bytes 196616 | tf_op jit(solution)/shard_map/while/body/eval_jaxpr/ppermute | solution.py:28
  190.1 6.4 %collective-permute-start.1 = (bf16[128,128]{1,0:T(8,128)(2,1)S(1)}, bf16[128,128]{1,0:T(8,128)(2,1)S(1)}, u32[]{:S(2)}, u32[]{:S(2)}) collective-permute-start(bf16[128,128]{1,0:T(8,128)(2,1)S(1)} %copy.84), channel_id=1, source_target_pairs={{0,1},{1,2},{2,3},{3,4},{4,5},{5,6},{6,7},{7,8},{8,9},{9,10},{10,1... | collective-permute-start | bytes 98312 | tf_op jit(solution)/shard_map/while/body/eval_jaxpr/ppermute | solution.py:28
  192.5 6.4 %collective-permute-start.2 = (f32[128,128]{1,0:T(8,128)S(1)}, f32[128,128]{1,0:T(8,128)S(1)}, u32[]{:S(2)}, u32[]{:S(2)}) collective-permute-start(f32[128,128]{1,0:T(8,128)S(1)} %fusion.123), channel_id=1, source_target_pairs={{0,1},{1,2},{2,3},{3,4},{4,5},{5,6},{6,7},{7,8},{8,9},{9,10},{10,1... | collective-permute-start | bytes 196616 | tf_op jit(solution)/shard_map/while/body/eval_jaxpr/ppermute | solution.py:28
  192.8 6.8 %collective-permute-start.3 = (f32[128,128]{1,0:T(8,128)S(1)}, f32[128,128]{1,0:T(8,128)S(1)}, u32[]{:S(2)}, u32[]{:S(2)}) collective-permute-start(f32[128,128]{1,0:T(8,128)S(1)} %convolution_add_fusion.6), channel_id=1, source_target_pairs={{0,1},{1,2},{2,3},{3,4},{4,5},{5,6},{6,7},{7,8},{8,9},{9,10},{10,1... | collective-permute-start | bytes 196616 | tf_op jit(solution)/shard_map/while/body/eval_jaxpr/ppermute | solution.py:28
  199.6 6.4 %collective-permute-start.1 = (bf16[128,128]{1,0:T(8,128)(2,1)S(1)}, bf16[128,128]{1,0:T(8,128)(2,1)S(1)}, u32[]{:S(2)}, u32[]{:S(2)}) collective-permute-start(bf16[128,128]{1,0:T(8,128)(2,1)S(1)} %copy.84), channel_id=1, source_target_pairs={{0,1},{1,2},{2,3},{3,4},{4,5},{5,6},{6,7},{7,8},{8,9},{9,10},{10,1... | collective-permute-start | bytes 98312 | tf_op jit(solution)/shard_map/while/body/eval_jaxpr/ppermute | solution.py:28
  202.0 6.4 %collective-permute-start.2 = (f32[128,128]{1,0:T(8,128)S(1)}, f32[128,128]{1,0:T(8,128)S(1)}, u32[]{:S(2)}, u32[]{:S(2)}) collective-permute-start(f32[128,128]{1,0:T(8,128)S(1)} %fusion.123), channel_id=1, source_target_pairs={{0,1},{1,2},{2,3},{3,4},{4,5},{5,6},{6,7},{7,8},{8,9},{9,10},{10,1... | collective-permute-start | bytes 196616 | tf_op jit(solution)/shard_map/while/body/eval_jaxpr/ppermute | solution.py:28
  202.3 6.8 %collective-permute-start.3 = (f32[128,128]{1,0:T(8,128)S(1)}, f32[128,128]{1,0:T(8,128)S(1)}, u32[]{:S(2)}, u32[]{:S(2)}) collective-permute-start(f32[128,128]{1,0:T(8,128)S(1)} %convolution_add_fusion.6), channel_id=1, source_target_pairs={{0,1},{1,2},{2,3},{3,4},{4,5},{5,6},{6,7},{7,8},{8,9},{9,10},{10,1... | collective-permute-start | bytes 196616 | tf_op jit(solution)/shard_map/while/body/eval_jaxpr/ppermute | solution.py:28
  209.2 6.4 %collective-permute-start.1 = (bf16[128,128]{1,0:T(8,128)(2,1)S(1)}, bf16[128,128]{1,0:T(8,128)(2,1)S(1)}, u32[]{:S(2)}, u32[]{:S(2)}) collective-permute-start(bf16[128,128]{1,0:T(8,128)(2,1)S(1)} %copy.84), channel_id=1, source_target_pairs={{0,1},{1,2},{2,3},{3,4},{4,5},{5,6},{6,7},{7,8},{8,9},{9,10},{10,1... | collective-permute-start | bytes 98312 | tf_op jit(solution)/shard_map/while/body/eval_jaxpr/ppermute | solution.py:28
  211.5 6.4 %collective-permute-start.2 = (f32[128,128]{1,0:T(8,128)S(1)}, f32[128,128]{1,0:T(8,128)S(1)}, u32[]{:S(2)}, u32[]{:S(2)}) collective-permute-start(f32[128,128]{1,0:T(8,128)S(1)} %fusion.123), channel_id=1, source_target_pairs={{0,1},{1,2},{2,3},{3,4},{4,5},{5,6},{6,7},{7,8},{8,9},{9,10},{10,1... | collective-permute-start | bytes 196616 | tf_op jit(solution)/shard_map/while/body/eval_jaxpr/ppermute | solution.py:28
  211.8 6.8 %collective-permute-start.3 = (f32[128,128]{1,0:T(8,128)S(1)}, f32[128,128]{1,0:T(8,128)S(1)}, u32[]{:S(2)}, u32[]{:S(2)}) collective-permute-start(f32[128,128]{1,0:T(8,128)S(1)} %convolution_add_fusion.6), channel_id=1, source_target_pairs={{0,1},{1,2},{2,3},{3,4},{4,5},{5,6},{6,7},{7,8},{8,9},{9,10},{10,1... | collective-permute-start | bytes 196616 | tf_op jit(solution)/shard_map/while/body/eval_jaxpr/ppermute | solution.py:28
  218.7 6.4 %collective-permute-start.1 = (bf16[128,128]{1,0:T(8,128)(2,1)S(1)}, bf16[128,128]{1,0:T(8,128)(2,1)S(1)}, u32[]{:S(2)}, u32[]{:S(2)}) collective-permute-start(bf16[128,128]{1,0:T(8,128)(2,1)S(1)} %copy.84), channel_id=1, source_target_pairs={{0,1},{1,2},{2,3},{3,4},{4,5},{5,6},{6,7},{7,8},{8,9},{9,10},{10,1... | collective-permute-start | bytes 98312 | tf_op jit(solution)/shard_map/while/body/eval_jaxpr/ppermute | solution.py:28
  221.1 6.4 %collective-permute-start.2 = (f32[128,128]{1,0:T(8,128)S(1)}, f32[128,128]{1,0:T(8,128)S(1)}, u32[]{:S(2)}, u32[]{:S(2)}) collective-permute-start(f32[128,128]{1,0:T(8,128)S(1)} %fusion.123), channel_id=1, source_target_pairs={{0,1},{1,2},{2,3},{3,4},{4,5},{5,6},{6,7},{7,8},{8,9},{9,10},{10,1... | collective-permute-start | bytes 196616 | tf_op jit(solution)/shard_map/while/body/eval_jaxpr/ppermute | solution.py:28
  221.4 6.8 %collective-permute-start.3 = (f32[128,128]{1,0:T(8,128)S(1)}, f32[128,128]{1,0:T(8,128)S(1)}, u32[]{:S(2)}, u32[]{:S(2)}) collective-permute-start(f32[128,128]{1,0:T(8,128)S(1)} %convolution_add_fusion.6), channel_id=1, source_target_pairs={{0,1},{1,2},{2,3},{3,4},{4,5},{5,6},{6,7},{7,8},{8,9},{9,10},{10,1... | collective-permute-start | bytes 196616 | tf_op jit(solution)/shard_map/while/body/eval_jaxpr/ppermute | solution.py:28
  228.2 6.4 %collective-permute-start.1 = (bf16[128,128]{1,0:T(8,128)(2,1)S(1)}, bf16[128,128]{1,0:T(8,128)(2,1)S(1)}, u32[]{:S(2)}, u32[]{:S(2)}) collective-permute-start(bf16[128,128]{1,0:T(8,128)(2,1)S(1)} %copy.84), channel_id=1, source_target_pairs={{0,1},{1,2},{2,3},{3,4},{4,5},{5,6},{6,7},{7,8},{8,9},{9,10},{10,1... | collective-permute-start | bytes 98312 | tf_op jit(solution)/shard_map/while/body/eval_jaxpr/ppermute | solution.py:28
  230.6 6.4 %collective-permute-start.2 = (f32[128,128]{1,0:T(8,128)S(1)}, f32[128,128]{1,0:T(8,128)S(1)}, u32[]{:S(2)}, u32[]{:S(2)}) collective-permute-start(f32[128,128]{1,0:T(8,128)S(1)} %fusion.123), channel_id=1, source_target_pairs={{0,1},{1,2},{2,3},{3,4},{4,5},{5,6},{6,7},{7,8},{8,9},{9,10},{10,1... | collective-permute-start | bytes 196616 | tf_op jit(solution)/shard_map/while/body/eval_jaxpr/ppermute | solution.py:28
  230.9 6.8 %collective-permute-start.3 = (f32[128,128]{1,0:T(8,128)S(1)}, f32[128,128]{1,0:T(8,128)S(1)}, u32[]{:S(2)}, u32[]{:S(2)}) collective-permute-start(f32[128,128]{1,0:T(8,128)S(1)} %convolution_add_fusion.6), channel_id=1, source_target_pairs={{0,1},{1,2},{2,3},{3,4},{4,5},{5,6},{6,7},{7,8},{8,9},{9,10},{10,1... | collective-permute-start | bytes 196616 | tf_op jit(solution)/shard_map/while/body/eval_jaxpr/ppermute | solution.py:28
  238.2 6.4 %collective-permute-start.20 = (f32[128,128]{1,0:T(8,128)S(1)}, f32[128,128]{1,0:T(8,128)S(1)}, u32[]{:S(2)}, u32[]{:S(2)}) collective-permute-start(f32[128,128]{1,0:T(8,128)S(1)} %convolution_add_fusion.2), channel_id=1, source_target_pairs={{0,1},{1,2},{2,3},{3,4},{4,5},{5,6},{6,7},{7,8},{8,9},{9,10},{10,1... | collective-permute-start | bytes 196616 | tf_op jit(solution)/shard_map/ppermute | solution.py:28
  238.7 6.7 %collective-permute-start.19 = (f32[128,128]{1,0:T(8,128)S(1)}, f32[128,128]{1,0:T(8,128)S(1)}, u32[]{:S(2)}, u32[]{:S(2)}) collective-permute-start(f32[128,128]{1,0:T(8,128)S(1)} %fusion.45), channel_id=1, source_target_pairs={{0,1},{1,2},{2,3},{3,4},{4,5},{5,6},{6,7},{7,8},{8,9},{9,10},{10,1... | collective-permute-start | bytes 196616 | tf_op jit(solution)/shard_map/ppermute | solution.py:28
  (33 other events, 207.8 us)
